TPU v7x, 128 devices: a whole 4x4x4 slice. The times are simulated.
128 devices in a mesh: grp: 4 (over x), seq: 32 (over y, z, core).
Axes of the slice: x: 4, y: 4, z: 4, core: 2. Of those that a mesh axis runs over, the one named last changes fastest.
Arguments:
- queries: bfloat16 [65536, 2048], P(('grp', 'seq')), may hold values from -6 to 6
- key_vectors: bfloat16 [65536, 2048], P(('grp', 'seq')), may hold values from -6 to 6
- value_vectors: bfloat16 [65536, 2048], P(('grp', 'seq')), may hold values from -6 to 6
- forward_output: bfloat16 [65536, 2048], P(('grp', 'seq')), may hold values from -6 to 6
- output_grad: bfloat16 [65536, 2048], P(('grp', 'seq')), may hold values from -6 to 6
- log_normalizer: float32 [16, 65536], P(None, ('grp', 'seq')), may hold values from -1 to 12
- piece_start: int32 [65536], P(('grp', 'seq')), may hold values from 0 to 65535, as said below
- bar_window: int32 [65536], P(('grp', 'seq')), may hold values from 32 to 512, as said below
Outputs:
- query_grad: bfloat16 [65536, 2048], P(('grp', 'seq'))
- key_grad: bfloat16 [65536, 2048], P(('grp', 'seq'))
- value_grad: bfloat16 [65536, 2048], P(('grp', 'seq'))
Inputs may be any that keep to these rules, and one draw needn't show every extreme that they name: piece_start[t] is the first position of the piece that holds token t: it never falls along the sequence, is at most t, and equals t exactly where a piece begins; positions 0 and 65535 begin pieces. `bar_window`: a multiple of 32, the same for all tokens of one piece; the piece at position 0 has 512.
All inputs are finite; a program needn't handle non-finite values.
Results may differ from a plain program's by a relative error of at most 0.0045.
The roundings to bfloat16 on the way count: a program that leaves them out, or rounds other values in their place, can miss the bound.
Values may be sent and summed in bfloat16 or wider, within the bound.
A program may use at most 256 MiB of HBM per device.

v0:
```python
import jax
import jax.numpy as jnp
from jax import lax
from jax.sharding import PartitionSpec as P


def passed_along(block, axis, distance):
    devices = range(lax.axis_size(axis))
    route = [(i - distance, i) for i in devices if i - distance in devices]
    return lax.ppermute(block, axis, route)


def visible_pairs(query_start, query_window, key_start, offset):
    grid_shape = (query_start.shape[0], key_start.shape[0])
    distance = (
        offset
        + lax.broadcasted_iota(jnp.int32, grid_shape, 0)
        - lax.broadcasted_iota(jnp.int32, grid_shape, 1)
    )
    same_piece = query_start[:, None] == key_start[None, :]
    return same_piece & (distance >= 0) & (distance < query_window[:, None])


def block_grads(queries, output_grad, normalizer, delta_rows, key_vectors, value_vectors, visible):
    head_count = normalizer.shape[0]
    model_width = queries.shape[1]
    head_size = model_width // head_count
    softmax_scale = head_size ** (-0.5)
    rows_here = queries.shape[0]
    columns = key_vectors.shape[0]
    query_heads = queries.reshape(rows_here, head_count, head_size)
    grad_heads = output_grad.reshape(rows_here, head_count, head_size)
    key_heads = key_vectors.reshape(columns, head_count, head_size)
    value_heads = value_vectors.reshape(columns, head_count, head_size)
    scores = (
        jnp.einsum("qhd,khd->hqk", query_heads, key_heads, preferred_element_type=jnp.float32)
        * softmax_scale
    )
    softmax_probs = jnp.where(visible[None], jnp.exp(scores - normalizer[:, :, None]), 0.0)
    prob_grad = jnp.einsum(
        "qhd,khd->hqk", grad_heads, value_heads, preferred_element_type=jnp.float32
    )
    score_grad = softmax_probs * (prob_grad - delta_rows[:, :, None])
    rounded_probs = softmax_probs.astype(jnp.bfloat16)
    rounded_grad = score_grad.astype(jnp.bfloat16)
    value_part = jnp.einsum(
        "hqk,qhd->khd", rounded_probs, grad_heads, preferred_element_type=jnp.float32
    )
    key_part = (
        jnp.einsum("hqk,qhd->khd", rounded_grad, query_heads, preferred_element_type=jnp.float32)
        * softmax_scale
    )
    query_part = (
        jnp.einsum("hqk,khd->qhd", rounded_grad, key_heads, preferred_element_type=jnp.float32)
        * softmax_scale
    )
    return (
        query_part.reshape(rows_here, model_width),
        key_part.reshape(columns, model_width),
        value_part.reshape(columns, model_width),
    )


def guarded(queries, output_grad, normalizer, delta_rows, key_vectors, value_vectors, visible):

    def compute(operands):
        return block_grads(*operands)

    def nothing(operands):
        model_width = queries.shape[1]
        return (
            jnp.zeros((queries.shape[0], model_width), jnp.float32),
            jnp.zeros((key_vectors.shape[0], model_width), jnp.float32),
            jnp.zeros((key_vectors.shape[0], model_width), jnp.float32),
        )

    operands = (queries, output_grad, normalizer, delta_rows, key_vectors, value_vectors, visible)
    return lax.cond(jnp.any(visible), compute, nothing, operands)


def local(
    queries,
    key_vectors,
    value_vectors,
    forward_output,
    output_grad,
    log_normalizer,
    piece_start,
    bar_window,
):
    rows_here, model_width = queries.shape
    head_count = log_normalizer.shape[0]
    head_size = model_width // head_count
    products = forward_output.astype(jnp.float32) * output_grad.astype(jnp.float32)
    delta_rows = jnp.sum(products.reshape(rows_here, head_count, head_size), axis=2).T
    local_part = guarded(
        queries,
        output_grad,
        log_normalizer,
        delta_rows,
        key_vectors,
        value_vectors,
        visible_pairs(piece_start, bar_window, piece_start, 0),
    )
    earlier_keys, earlier_values, earlier_start = passed_along(
        (key_vectors, value_vectors, piece_start), ("grp", "seq"), 1
    )
    shared_part = guarded(
        queries,
        output_grad,
        log_normalizer,
        delta_rows,
        earlier_keys,
        earlier_values,
        visible_pairs(piece_start, bar_window, earlier_start, rows_here),
    )
    returned_keys, returned_values = (
        passed_along(shared_part[1].astype(jnp.bfloat16), ("grp", "seq"), -1).astype(jnp.float32),
        passed_along(shared_part[2].astype(jnp.bfloat16), ("grp", "seq"), -1).astype(jnp.float32),
    )
    query_total = local_part[0] + shared_part[0]
    key_total = local_part[1] + returned_keys
    value_total = local_part[2] + returned_values
    return (
        query_total.astype(jnp.bfloat16),
        key_total.astype(jnp.bfloat16),
        value_total.astype(jnp.bfloat16),
    )


def solution(mesh):
    placed = (
        P(("grp", "seq"), None),
        P(("grp", "seq"), None),
        P(("grp", "seq"), None),
        P(("grp", "seq"), None),
        P(("grp", "seq"), None),
        P(None, ("grp", "seq")),
        P(("grp", "seq")),
        P(("grp", "seq")),
    )
    return jax.shard_map(
        local,
        mesh=mesh,
        in_specs=placed,
        out_specs=(P(("grp", "seq"), None), P(("grp", "seq"), None), P(("grp", "seq"), None)),
        check_vma=False,
    )
```

profile of v0, /device:TPU:6, one launch (start us, length us, event | category | flops | bytes accessed | tf_op | source)
XLA Modules:
  0.0 209.7 jit_solution(10291945830537331095)
XLA Ops:
  21.1 38.2 %collective-permute-done = s32[512]{0:T(512)S(1)} collective-permute-done((s32[512]{0:T(512)S(1)}, s32[512]{0:T(512)S(1)}, u32[]{:S(2)}, u32[]{:S(2)}) %collective-permute-start) | collective-permute-done | bytes 2080 | tf_op jit(solution)/shard_map/ppermute | solution.py:10
  61.6 51.9 %conditional.3 = (bf16[512,2048]{0,1:T(8,128)(2,1)}, bf16[512,2048]{0,1:T(8,128)(2,1)}, f32[512,2048]{1,0:T(8,128)}) conditional(s32[]{:T(128)} %convert_element_type.48, () %tuple.26, (pred[512,512]{1,0:T(8,128)(4,1)S(1)}, bf16[512,2048]{1,0:T(8,128)(2,1)}, bf16[512,2048]{0,1:T(8,128)(2,1)}, f32[16,512]{1,0:T(8,128)S(1)}, ...), branch_computations={%region_5.6_spmd, %region_6.7_spmd} | conditional | flops 5413797888 | bytes 225083520 | solution.py:78
  67.3 4.1 %fusion.34 = f32[16,512,512]{2,1,0:T(8,128)S(1)} fusion(bf16[512,16,128]{0,2,1:T(8,128)(2,1)S(1)} %bitcast.58, bf16[512,16,128]{0,2,1:T(8,128)(2,1)} %bitcast.10), kind=kOutput, calls=%fused_computation.46 | convolution fusion | flops 1073741824 | bytes 20971520 | tf_op jit(solution)/shard_map/cond/branch_1_fun/qhd,khd->hqk/dot_general | solution.py:36
  71.4 5.7 %copy-done.5 = f32[16,512,512]{2,1,0:T(8,128)} copy-done((f32[16,512,512]{2,1,0:T(8,128)}, f32[16,512,512]{2,1,0:T(8,128)S(1)}, u32[]{:S(2)}) %copy-start.5) | copy-done | bytes 16777240 | tf_op jit(solution)/shard_map/cond
  77.1 5.5 %fusion.12 = bf16[16,512,128]{1,2,0:T(8,128)(2,1)} fusion(bf16[512,16,128]{0,2,1:T(8,128)(2,1)S(1)} %bitcast.73, f32[16,512,512]{2,1,0:T(8,128)S(1)} %fusion.34, f32[16,512]{1,0:T(8,128)S(1)} %get-tuple-element.38, pred[512,512]{1,0:T(8,128)(4,1)S(1)} %get-tuple-element.35), kind=kOutput, calls=%fused_computation.17 | convolution fusion | flops 1090519040 | bytes 21266432 | tf_op jit(solution)/shard_map/cond/branch_1_fun/hqk,qhd->khd/dot_general | solution.py:46
  82.7 13.0 %multiply_convert_fusion.1 = bf16[16,512,512]{2,1,0:T(8,128)(2,1)} fusion(f32[16,512,512]{2,1,0:T(8,128)} %copy-done.5, bf16[512,16,128]{0,2,1:T(8,128)(2,1)S(1)} %bitcast.74, f32[16,512]{1,0:T(8,128)S(1)} %copy.46, f32[16,512]{1,0:T(8,128)S(1)} %get-tuple-element.38, pred[512,512]{1,0:T(8,128)(4,1)S(1)} %get-tuple-element.35, ...), kind=kOutput, calls=%fused_computation.14 | convolution fusion | flops 1098907648 | bytes 29687808 | tf_op jit(solution)/shard_map/cond/branch_1_fun/qhd,khd->hqk/dot_general | solution.py:40
  95.7 6.1 %convolution_multiply_fusion.2 = bf16[16,512,128]{1,2,0:T(8,128)(2,1)} fusion(bf16[512,16,128]{0,2,1:T(8,128)(2,1)S(1)} %bitcast.59, bf16[16,512,512]{2,1,0:T(8,128)(2,1)} %multiply_convert_fusion.1), kind=kOutput, calls=%fused_computation.22 | convolution fusion | flops 1075838976 | bytes 12582912 | tf_op jit(solution)/shard_map/cond/branch_1_fun/hqk,qhd->khd/dot_general | solution.py:50
  101.8 6.4 %convolution_multiply_fusion.3 = f32[16,512,128]{1,2,0:T(8,128)} fusion(bf16[16,512,512]{2,1,0:T(8,128)(2,1)S(1)} %copy-done, bf16[512,16,128]{0,2,1:T(8,128)(2,1)} %bitcast.10), kind=kOutput, calls=%fused_computation.23 | convolution fusion | flops 1074790400 | bytes 14680064 | tf_op jit(solution)/shard_map/cond/branch_1_fun/hqk,khd->qhd/dot_general | solution.py:54
  108.2 5.4 %copy.66 = f32[512,2048]{1,0:T(8,128)} copy(f32[512,2048]{0,1:T(8,128)} %bitcast.66) | data formatting | bytes 8388608 | tf_op jit(solution)/shard_map/cond | solution.py:78
  113.5 4.1 %copy.51 = bf16[512,2048]{1,0:T(8,128)(2,1)} copy(bf16[512,2048]{0,1:T(8,128)(2,1)} %get-tuple-element.56) | data formatting | bytes 4194304 | tf_op jit(solution)/shard_map/cond | solution.py:78
  123.5 4.3 %collective-permute-start.3 = (bf16[512,2048]{1,0:T(8,128)(2,1)}, bf16[512,2048]{1,0:T(8,128)(2,1)}, u32[]{:S(2)}, u32[]{:S(2)}) collective-permute-start(bf16[512,2048]{1,0:T(8,128)(2,1)} %copy.49), channel_id=1, source_target_pairs={{1,0},{2,1},{3,2},{4,3},{5,4},{6,5},{7,6},{8,7},{9,8},{10,9},{11,1... | collective-permute-start | bytes 6291464 | tf_op jit(solution)/shard_map/ppermute | solution.py:10
  128.5 66.0 %conditional.2 = (f32[512,2048]{1,0:T(8,128)}, f32[512,2048]{1,0:T(8,128)}, f32[512,2048]{1,0:T(8,128)}) conditional(s32[]{:T(128)} %convert_element_type.45, () %tuple.24, (pred[512,512]{1,0:T(8,128)(4,1)S(1)}, bf16[512,2048]{1,0:T(8,128)(2,1)}, bf16[512,2048]{1,0:T(8,128)(2,1)}, f32[16,512]{1,0:T(8,128)S(1)}, bf16[512,2048]{1,0:T(8,128)(2,1)S(1)}, ...), branch_computations={%region_2.0_spmd, %region_3.4_spmd} | conditional | flops 5412749312 | bytes 267026624 | solution.py:78
  138.1 4.1 %fusion.33 = f32[16,512,512]{2,1,0:T(8,128)S(1)} fusion(bf16[512,16,128]{0,2,1:T(8,128)(2,1)S(1)} %bitcast.61, bf16[512,16,128]{0,2,1:T(8,128)(2,1)} %bitcast.63), kind=kOutput, calls=%fused_computation.45 | convolution fusion | flops 1073741824 | bytes 20971520 | tf_op jit(solution)/shard_map/cond/branch_1_fun/qhd,khd->hqk/dot_general | solution.py:36
  142.2 5.7 %copy-done.6 = f32[16,512,512]{2,1,0:T(8,128)} copy-done((f32[16,512,512]{2,1,0:T(8,128)}, f32[16,512,512]{2,1,0:T(8,128)S(1)}, u32[]{:S(2)}) %copy-start.6) | copy-done | bytes 16777240 | tf_op jit(solution)/shard_map/cond
  148.0 5.5 %fusion.1 = f32[16,512,128]{1,2,0:T(8,128)} fusion(bf16[512,16,128]{0,2,1:T(8,128)(2,1)S(1)} %bitcast.71, f32[16,512,512]{2,1,0:T(8,128)S(1)} %fusion.33, f32[16,512]{1,0:T(8,128)S(1)} %get-tuple-element.31, pred[512,512]{1,0:T(8,128)(4,1)S(1)} %get-tuple-element.28), kind=kOutput, calls=%fused_computation.3 | convolution fusion | flops 1090519040 | bytes 23363584 | tf_op jit(solution)/shard_map/cond/branch_1_fun/hqk,qhd->khd/dot_general | solution.py:46
  153.5 12.3 %multiply_convert_fusion = bf16[16,512,512]{2,1,0:T(8,128)(2,1)} fusion(f32[16,512,512]{2,1,0:T(8,128)} %copy-done.6, bf16[512,16,128]{0,2,1:T(8,128)(2,1)S(1)} %bitcast.72, f32[16,512]{1,0:T(8,128)S(1)} %copy.42, f32[16,512]{1,0:T(8,128)S(1)} %get-tuple-element.31, pred[512,512]{1,0:T(8,128)(4,1)S(1)} %get-tuple-element.28, bf16[512,2048]{1,0:T(8,128)(2,1)S(1)} %copy-done.11), kind=kOutput, calls=%fused_computation | convolution fusion | flops 1098907648 | bytes 29687808 | tf_op jit(solution)/shard_map/cond/branch_1_fun/qhd,khd->hqk/dot_general | solution.py:40
  165.7 5.4 %copy.64 = f32[512,2048]{1,0:T(8,128)} copy(f32[512,2048]{0,1:T(8,128)} %bitcast.68) | data formatting | bytes 8388608 | tf_op jit(solution)/shard_map/cond | solution.py:78
  171.1 6.9 %convolution_multiply_fusion = f32[16,512,128]{1,2,0:T(8,128)} fusion(bf16[512,16,128]{0,2,1:T(8,128)(2,1)S(1)} %bitcast.62, bf16[16,512,512]{2,1,0:T(8,128)(2,1)} %multiply_convert_fusion), kind=kOutput, calls=%fused_computation.8 | convolution fusion | flops 1074790400 | bytes 14680064 | tf_op jit(solution)/shard_map/cond/branch_1_fun/hqk,qhd->khd/dot_general | solution.py:50
  178.9 4.8 %convolution_multiply_fusion.1 = f32[16,512,128]{1,2,0:T(8,128)} fusion(bf16[16,512,512]{2,1,0:T(8,128)(2,1)S(1)} %copy-done.1, bf16[512,16,128]{0,2,1:T(8,128)(2,1)S(1)} %bitcast.64), kind=kOutput, calls=%fused_computation.9 | convolution fusion | flops 1074790400 | bytes 14680064 | tf_op jit(solution)/shard_map/cond/branch_1_fun/hqk,khd->qhd/dot_general | solution.py:54
  183.7 5.4 %copy.60 = f32[512,2048]{1,0:T(8,128)} copy(f32[512,2048]{0,1:T(8,128)} %bitcast.65) | data formatting | bytes 8388608 | tf_op jit(solution)/shard_map/cond | solution.py:78
  189.1 5.4 %copy.62 = f32[512,2048]{1,0:T(8,128)} copy(f32[512,2048]{0,1:T(8,128)} %bitcast.60) | data formatting | bytes 8388608 | tf_op jit(solution)/shard_map/cond | solution.py:78
  194.4 5.4 %add_convert_fusion.2 = bf16[512,2048]{1,0:T(8,128)(2,1)} fusion(f32[512,2048]{1,0:T(8,128)} %get-tuple-element.85, f32[512,2048]{1,0:T(8,128)} %get-tuple-element.88), kind=kLoop, calls=%fused_computation.30 | loop fusion | flops 2097152 | bytes 10485760 | tf_op jit(solution)/shard_map/convert_element_type | solution.py:125
  199.9 4.9 %add_convert_fusion = bf16[512,2048]{1,0:T(8,128)(2,1)} fusion(f32[512,2048]{1,0:T(8,128)} %get-tuple-element.87, bf16[512,2048]{1,0:T(8,128)(2,1)} %collective-permute-done.4), kind=kLoop, calls=%fused_computation.28 | loop fusion | flops 3145728 | bytes 8388608 | tf_op jit(solution)/shard_map/convert_element_type | solution.py:127
  204.8 4.9 %add_convert_fusion.1 = bf16[512,2048]{1,0:T(8,128)(2,1)} fusion(f32[512,2048]{1,0:T(8,128)} %get-tuple-element.86, bf16[512,2048]{1,0:T(8,128)(2,1)} %collective-permute-done.3), kind=kLoop, calls=%fused_computation.29 | loop fusion | flops 3145728 | bytes 8388608 | tf_op jit(solution)/shard_map/convert_element_type | solution.py:126
  (46 shorter events, 43.6 us)
Async XLA Ops:
  0.6 10.0 %copy-start.9 = (s32[512]{0:T(512)S(1)}, s32[512]{0:T(512)}, u32[]{:S(2)}) copy-start(s32[512]{0:T(512)} %param.18) | copy-start | bytes 6148
  0.6 11.9 %copy-start.3 = (bf16[512,2048]{1,0:T(8,128)(2,1)S(1)}, bf16[512,2048]{1,0:T(8,128)(2,1)}, u32[]{:S(2)}) copy-start(bf16[512,2048]{1,0:T(8,128)(2,1)} %param.16) | copy-start | bytes 6291460
  4.7 56.9 %collective-permute-start.1 = (bf16[512,2048]{0,1:T(8,128)(2,1)}, bf16[512,2048]{0,1:T(8,128)(2,1)}, u32[]{:S(2)}, u32[]{:S(2)}) collective-permute-start(bf16[512,2048]{0,1:T(8,128)(2,1)} %copy.43), channel_id=1, source_target_pairs={{0,1},{1,2},{2,3},{3,4},{4,5},{5,6},{6,7},{7,8},{8,9},{9,10},{10,1... | collective-permute-start | bytes 6291464 | tf_op jit(solution)/shard_map/ppermute | solution.py:10
  6.6 54.9 %collective-permute-start.2 = (bf16[512,2048]{1,0:T(8,128)(2,1)}, bf16[512,2048]{1,0:T(8,128)(2,1)}, u32[]{:S(2)}, u32[]{:S(2)}) collective-permute-start(bf16[512,2048]{1,0:T(8,128)(2,1)} %param.14), channel_id=1, source_target_pairs={{0,1},{1,2},{2,3},{3,4},{4,5},{5,6},{6,7},{7,8},{8,9},{9,10},{10,1... | collective-permute-start | bytes 6291464 | tf_op jit(solution)/shard_map/ppermute | solution.py:10
  10.6 48.7 %collective-permute-start = (s32[512]{0:T(512)S(1)}, s32[512]{0:T(512)S(1)}, u32[]{:S(2)}, u32[]{:S(2)}) collective-permute-start(s32[512]{0:T(512)S(1)} %copy-done.9), channel_id=1, source_target_pairs={{0,1},{1,2},{2,3},{3,4},{4,5},{5,6},{6,7},{7,8},{8,9},{9,10},{10,1... | collective-permute-start | bytes 6152 | tf_op jit(solution)/shard_map/ppermute | solution.py:10
  17.8 41.6 %copy-start.10 = (s32[512]{0:T(512)S(1)}, s32[512]{0:T(512)}, u32[]{:S(2)}) copy-start(s32[512]{0:T(512)} %param.19) | copy-start | bytes 6148
  17.8 43.8 %copy-start.12 = (f32[16,512]{1,0:T(8,128)S(1)}, f32[16,512]{1,0:T(8,128)}, u32[]{:S(2)}) copy-start(f32[16,512]{1,0:T(8,128)} %param.17) | copy-start | bytes 98308
  67.3 9.9 %copy-start.8 = (bf16[512,2048]{0,1:T(8,128)(2,1)S(1)}, bf16[512,2048]{0,1:T(8,128)(2,1)}, u32[]{:S(2)}) copy-start(bf16[512,2048]{0,1:T(8,128)(2,1)} %copy.45) | copy-start | bytes 6291460 | tf_op jit(solution)/shard_map/cond
  71.4 5.7 %copy-start.5 = (f32[16,512,512]{2,1,0:T(8,128)}, f32[16,512,512]{2,1,0:T(8,128)S(1)}, u32[]{:S(2)}) copy-start(f32[16,512,512]{2,1,0:T(8,128)S(1)} %fusion.34) | copy-start | bytes 50331652 | tf_op jit(solution)/shard_map/cond
  95.7 6.1 %copy-start = (bf16[16,512,512]{2,1,0:T(8,128)(2,1)S(1)}, bf16[16,512,512]{2,1,0:T(8,128)(2,1)}, u32[]{:S(2)}) copy-start(bf16[16,512,512]{2,1,0:T(8,128)(2,1)} %multiply_convert_fusion.1) | copy-start | bytes 25165828 | tf_op jit(solution)/shard_map/cond
  113.5 14.9 %copy-start.4 = (bf16[512,2048]{1,0:T(8,128)(2,1)S(1)}, bf16[512,2048]{1,0:T(8,128)(2,1)}, u32[]{:S(2)}) copy-start(bf16[512,2048]{1,0:T(8,128)(2,1)} %param.16) | copy-start | bytes 6291460
  117.7 82.2 %collective-permute-start.4 = (bf16[512,2048]{1,0:T(8,128)(2,1)}, bf16[512,2048]{1,0:T(8,128)(2,1)}, u32[]{:S(2)}, u32[]{:S(2)}) collective-permute-start(bf16[512,2048]{1,0:T(8,128)(2,1)} %copy.51), channel_id=1, source_target_pairs={{1,0},{2,1},{3,2},{4,3},{5,4},{6,5},{7,6},{8,7},{9,8},{10,9},{11,1... | collective-permute-start | bytes 6291464 | tf_op jit(solution)/shard_map/ppermute | solution.py:10
  123.5 81.3 %collective-permute-start.3 = (bf16[512,2048]{1,0:T(8,128)(2,1)}, bf16[512,2048]{1,0:T(8,128)(2,1)}, u32[]{:S(2)}, u32[]{:S(2)}) collective-permute-start(bf16[512,2048]{1,0:T(8,128)(2,1)} %copy.49), channel_id=1, source_target_pairs={{1,0},{2,1},{3,2},{4,3},{5,4},{6,5},{7,6},{8,7},{9,8},{10,9},{11,1... | collective-permute-start | bytes 6291464 | tf_op jit(solution)/shard_map/ppermute | solution.py:10
  138.1 9.9 %copy-start.7 = (bf16[512,2048]{0,1:T(8,128)(2,1)S(1)}, bf16[512,2048]{0,1:T(8,128)(2,1)}, u32[]{:S(2)}) copy-start(bf16[512,2048]{0,1:T(8,128)(2,1)} %copy.41) | copy-start | bytes 6291460 | tf_op jit(solution)/shard_map/cond
  142.2 5.7 %copy-start.6 = (f32[16,512,512]{2,1,0:T(8,128)}, f32[16,512,512]{2,1,0:T(8,128)S(1)}, u32[]{:S(2)}) copy-start(f32[16,512,512]{2,1,0:T(8,128)S(1)} %fusion.33) | copy-start | bytes 50331652 | tf_op jit(solution)/shard_map/cond
  148.0 5.5 %copy-start.11 = (bf16[512,2048]{1,0:T(8,128)(2,1)S(1)}, bf16[512,2048]{1,0:T(8,128)(2,1)}, u32[]{:S(2)}) copy-start(bf16[512,2048]{1,0:T(8,128)(2,1)} %get-tuple-element.33) | copy-start | bytes 6291460 | tf_op jit(solution)/shard_map/cond
  171.1 6.9 %copy-start.1 = (bf16[16,512,512]{2,1,0:T(8,128)(2,1)S(1)}, bf16[16,512,512]{2,1,0:T(8,128)(2,1)}, u32[]{:S(2)}) copy-start(bf16[16,512,512]{2,1,0:T(8,128)(2,1)} %multiply_convert_fusion) | copy-start | bytes 25165828 | tf_op jit(solution)/shard_map/cond
  171.1 7.8 %copy-start.2 = (bf16[512,2048]{0,1:T(8,128)(2,1)S(1)}, bf16[512,2048]{0,1:T(8,128)(2,1)}, u32[]{:S(2)}) copy-start(bf16[512,2048]{0,1:T(8,128)(2,1)} %copy.40) | copy-start | bytes 6291460 | tf_op jit(solution)/shard_map/cond
where the time goes:
time: 211 us; the launch traced here: 210 us
  matrix products  68.7 us (33%)
  local copies, waits for them, and re-layouts  63.7 us (30%)
  waiting for transfers between devices  38.2 us (18%)
  other arithmetic  22.5 us (11%)
  starting transfers between devices  14 us (7%)
    ppermute x5, waiting for transfers between devices, passed_along(): return lax.ppermute(block, axis, route)  38.2 us
    cond x6, local copies, waits for them, and re-layouts, guarded(): return lax.cond(jnp.any(visible), compute, nothing, operands)  29.5 us
    dot_general x2, matrix products, block_grads(): jnp.einsum('qhd,khd->hqk', grad_heads, value_heads, preferred_element_typ...  25.3 us
    another operation x7, local copies, waits for them, and re-layouts  14.8 us
    ppermute x5, starting transfers between devices, passed_along(): return lax.ppermute(block, axis, route)  14 us
    dot_general x2, matrix products, block_grads(): jnp.einsum('hqk,qhd->khd', rounded_grad, query_heads, preferred_element_t...  13 us
    cond x16, local copies, waits for them, and re-layouts  12.4 us
    dot_general x2, matrix products, block_grads(): jnp.einsum('hqk,khd->qhd', rounded_grad, key_heads, preferred_element_typ...  11.2 us
  transfers between devices with their start and end apart: 5, of which 1 were waited for; matrix products, arithmetic and copies ran while one was open for 40% of the time, Pallas kernels for 0%

commit v1 on v0

v1 whole, which is shorter than its diff:
```python
import functools

import jax
import jax.numpy as jnp
from jax import lax
from jax.experimental import pallas as pl
from jax.experimental.pallas import tpu as pltpu
from jax.sharding import PartitionSpec as P

MESH = pl.DeviceIdType.MESH
LOG2E = 1.4426950408889634
HEAD = 128
LAG = 3
AHEAD = 2


def dot(a, b, contract):
    return lax.dot_general(
        a, b, ((contract[:1], contract[1:]), ((), ())), preferred_element_type=jnp.float32
    )


def kernel(
    groups,
    group_size,
    heads,
    q_hbm,
    k_hbm,
    v_hbm,
    o_hbm,
    g_hbm,
    lse_hbm,
    start_hbm,
    window_hbm,
    dq_out,
    dk_out,
    dv_out,
    q_own,
    k_own,
    v_own,
    o_own,
    g_own,
    lse_own,
    start_own,
    window_own,
    stats_own,
    stats_next,
    q_next,
    g_next,
    dq_own,
    dq_sent,
    dq_got,
    load_sem,
    send_sem,
    recv_sem,
    stats_sem,
    back_send_sem,
    back_recv_sem,
):
    rows = q_hbm.shape[0]
    half = rows // 2
    count = groups * group_size
    here = lax.axis_index("grp") * group_size + lax.axis_index("seq")

    def place(index):
        return (index // group_size, lax.rem(index, group_size))

    before = place(lax.rem(here + count - 1, count))
    after = place(lax.rem(here + 1, count))

    def load(number, source, target):
        return pltpu.make_async_copy(source, target, load_sem.at[number])

    loads = [
        load(0, o_hbm, o_own),
        load(1, g_hbm, g_own),
        load(2, lse_hbm, lse_own),
        load(3, start_hbm, start_own),
        load(4, window_hbm, window_own),
        load(5, q_hbm, q_own),
        load(6, k_hbm, k_own),
        load(7, v_hbm, v_own),
    ]
    for copy in loads:
        copy.start()

    barrier = pltpu.get_barrier_semaphore()
    for neighbour in (before, after):
        pl.semaphore_signal(barrier, inc=1, device_id=neighbour, device_id_type=MESH)
    pl.semaphore_wait(barrier, 2)

    def columns(h):
        return pl.ds(pl.multiple_of(h * HEAD, HEAD), HEAD)

    def to_before(h):
        return [
            pltpu.make_async_remote_copy(
                src_ref=source.at[:, columns(h)],
                dst_ref=target.at[h],
                send_sem=send_sem.at[number, h],
                recv_sem=recv_sem.at[number, h],
                device_id=before,
                device_id_type=MESH,
            )
            for number, (source, target) in enumerate(((q_hbm, q_next), (g_hbm, g_next)))
        ]

    def to_after(h):
        return pltpu.make_async_remote_copy(
            src_ref=dq_sent.at[h],
            dst_ref=dq_got.at[h],
            send_sem=back_send_sem.at[h],
            recv_sem=back_recv_sem.at[h],
            device_id=after,
            device_id_type=MESH,
        )

    for h in range(AHEAD):
        for copy in to_before(h):
            copy.start()

    for copy in loads[:5]:
        copy.wait()
    positions = lax.broadcasted_iota(jnp.int32, (1, rows), 1)
    lowest = (
        jnp.maximum(
            start_own[...].reshape(1, rows) - here * rows,
            positions - window_own[...].reshape(1, rows) + 1,
        )
    ).astype(jnp.float32)
    stats_own[0:heads, :] = lse_own[...] * LOG2E
    model = heads * HEAD
    picks = (
        lax.broadcasted_iota(jnp.int32, (heads, model), 1) // HEAD
        == lax.broadcasted_iota(jnp.int32, (heads, model), 0)
    ).astype(jnp.float32).astype(jnp.bfloat16)
    for r in range(0, rows, 128):
        products = o_own[r : r + 128, :].astype(jnp.float32) * g_own[r : r + 128, :].astype(
            jnp.float32
        )
        high = products.astype(jnp.bfloat16)
        low = (products - high.astype(jnp.float32)).astype(jnp.bfloat16)
        stats_own[heads : 2 * heads, r : r + 128] = dot(picks, high, (1, 1)) + dot(
            picks, low, (1, 1)
        )
    stats_own[2 * heads : 2 * heads + 8, :] = jnp.broadcast_to(lowest + rows, (8, rows))
    stats_copy = pltpu.make_async_remote_copy(
        src_ref=stats_own,
        dst_ref=stats_next,
        send_sem=stats_sem.at[0],
        recv_sem=stats_sem.at[1],
        device_id=before,
        device_id_type=MESH,
    )
    stats_copy.start()
    for copy in loads[5:]:
        copy.wait()

    scale = HEAD**-0.5

    def pair_block(k, v, q, g, lse, delta, mask):
        s = dot(k, q, (1, 1)) * (scale * LOG2E) - lse
        p = jnp.where(mask, jnp.exp2(s), 0.0)
        ds = p * (dot(v, g, (1, 1)) - delta)
        return p.astype(jnp.bfloat16), ds.astype(jnp.bfloat16)

    def finish(h):
        to_after(h).wait_recv()
        total = dq_own[h] + dq_got[h].astype(jnp.float32)
        dq_out[:, columns(h)] = total.T.astype(jnp.bfloat16)

    key_at = lax.broadcasted_iota(jnp.int32, (half, half), 0).astype(jnp.float32)
    query_at = lax.broadcasted_iota(jnp.int32, (half, half), 1).astype(jnp.float32)
    lo, hi = slice(0, half), slice(half, rows)

    def one_head(h, carry):
        @pl.when(h + AHEAD < heads)
        def _():
            for copy in to_before(h):
                copy.wait_send()
            for copy in to_before(h + AHEAD):
                copy.start()

        cols = columns(h)
        k, v, q, g = k_own[:, cols], v_own[:, cols], q_own[:, cols], g_own[:, cols]
        kt = k.T
        lse = stats_own[pl.ds(h, 1), :]
        delta = stats_own[pl.ds(heads + h, 1), :]
        bound = stats_own[2 * heads : 2 * heads + 1, :] - rows

        def local(us, ts, diagonal):
            mask = key_at + us.start >= bound[:, ts]
            if diagonal:
                mask = mask & (key_at <= query_at)
            return pair_block(k[us], v[us], q[ts], g[ts], lse[:, ts], delta[:, ts], mask)

        p00, s00 = local(lo, lo, True)
        p01, s01 = local(lo, hi, False)
        p11, s11 = local(hi, hi, True)
        dv0 = dot(p00, g[lo], (1, 0)) + dot(p01, g[hi], (1, 0))
        dv1 = dot(p11, g[hi], (1, 0))
        dk0 = dot(s00, q[lo], (1, 0)) + dot(s01, q[hi], (1, 0))
        dk1 = dot(s11, q[hi], (1, 0))
        dq_own[h, :, lo] = dot(kt[:, lo], s00, (1, 0)) * scale
        dq_own[h, :, hi] = (dot(kt[:, lo], s01, (1, 0)) + dot(kt[:, hi], s11, (1, 0))) * scale

        @pl.when(h == 0)
        def _():
            stats_copy.wait_recv()

        for copy in to_before(h):
            copy.wait_recv()
        qn, gn = q_next[h], g_next[h]
        lse_n = stats_next[pl.ds(h, 1), :]
        delta_n = stats_next[pl.ds(heads + h, 1), :]
        bound_n = stats_next[2 * heads : 2 * heads + 1, :]

        def shared(us, ts):
            mask = key_at + us.start >= bound_n[:, ts]
            return pair_block(k[us], v[us], qn[ts], gn[ts], lse_n[:, ts], delta_n[:, ts], mask)

        p00, s00 = shared(lo, lo)
        p10, s10 = shared(hi, lo)
        p11, s11 = shared(hi, hi)
        dq_sent[h, :, lo] = (
            (dot(kt[:, lo], s00, (1, 0)) + dot(kt[:, hi], s10, (1, 0))) * scale
        ).astype(jnp.bfloat16)
        dq_sent[h, :, hi] = (dot(kt[:, hi], s11, (1, 0)) * scale).astype(jnp.bfloat16)
        to_after(h).start()
        dv0 += dot(p00, gn[lo], (1, 0))
        dv1 += dot(p10, gn[lo], (1, 0)) + dot(p11, gn[hi], (1, 0))
        dk0 += dot(s00, qn[lo], (1, 0))
        dk1 += dot(s10, qn[lo], (1, 0)) + dot(s11, qn[hi], (1, 0))
        dv_out[lo, cols] = dv0.astype(jnp.bfloat16)
        dv_out[hi, cols] = dv1.astype(jnp.bfloat16)
        dk_out[lo, cols] = (dk0 * scale).astype(jnp.bfloat16)
        dk_out[hi, cols] = (dk1 * scale).astype(jnp.bfloat16)

        @pl.when(h >= LAG)
        def _():
            finish(h - LAG)

        return carry

    lax.fori_loop(0, heads, one_head, 0)
    lax.fori_loop(heads - LAG, heads, lambda h, c: (finish(h), c)[1], 0)
    stats_copy.wait_send()

    def drain(h, carry):
        to_after(h).wait_send()

        @pl.when(h + AHEAD >= heads)
        def _():
            for copy in to_before(h):
                copy.wait_send()

        return carry

    lax.fori_loop(0, heads, drain, 0)


def solution(mesh):
    groups, group_size = mesh.shape["grp"], mesh.shape["seq"]

    def local(q, k, v, o, g, lse, start, window):
        rows, model = q.shape
        heads = lse.shape[0]
        block = jax.ShapeDtypeStruct((rows, model), jnp.bfloat16)
        whole = pltpu.VMEM((rows, model), jnp.bfloat16)
        per_head = pltpu.VMEM((heads, rows, HEAD), jnp.bfloat16)
        turned = pltpu.VMEM((heads, HEAD, rows), jnp.bfloat16)
        stats = pltpu.VMEM((2 * heads + 8, rows), jnp.float32)
        return pl.pallas_call(
            functools.partial(kernel, groups, group_size, heads),
            out_shape=(block, block, block),
            in_specs=[pl.BlockSpec(memory_space=pl.ANY)] * 8,
            out_specs=(pl.BlockSpec(memory_space=pltpu.VMEM),) * 3,
            scratch_shapes=[
                whole,
                whole,
                whole,
                whole,
                whole,
                pltpu.VMEM((heads, rows), jnp.float32),
                pltpu.VMEM((rows,), jnp.int32),
                pltpu.VMEM((rows,), jnp.int32),
                stats,
                stats,
                per_head,
                per_head,
                pltpu.VMEM((heads, HEAD, rows), jnp.float32),
                turned,
                turned,
                pltpu.SemaphoreType.DMA((8,)),
                pltpu.SemaphoreType.DMA((2, heads)),
                pltpu.SemaphoreType.DMA((2, heads)),
                pltpu.SemaphoreType.DMA((2,)),
                pltpu.SemaphoreType.DMA((heads,)),
                pltpu.SemaphoreType.DMA((heads,)),
            ],
            compiler_params=pltpu.CompilerParams(
                collective_id=0, has_side_effects=True, vmem_limit_bytes=56 * 2**20
            ),
        )(q, k, v, o, g, lse, start, window)

    block = P(("grp", "seq"), None)
    return jax.shard_map(
        local,
        mesh=mesh,
        in_specs=(block,) * 5 + (P(None, ("grp", "seq")),) + (P(("grp", "seq")),) * 2,
        out_specs=(block,) * 3,
        check_vma=False,
    )
```

time: 211 us -> 78.3 us (0.37)
  the two profiles are of different devices: /device:TPU:6 before, /device:TPU:0 now
where the time goes in v1:
time: 78.3 us; the launch traced here: 78.2 us
  Pallas kernels  70.5 us (90%)
  local copies, waits for them, and re-layouts  6.98 us (9%)
    pallas_call x1, Pallas kernels, local(): pl.pallas_call(functools.partial(kernel, groups, group_size, heads), out_...  70.5 us
    unnamed x7, local copies, waits for them, and re-layouts  6.98 us

profile of v1, /device:TPU:0, one launch (start us, length us, event | category | flops | bytes accessed | tf_op | source)
XLA Modules:
  0.0 78.2 jit_solution(1188358751800681545)
XLA Ops:
  0.6 70.5 %shard_map.103 = (bf16[512,2048]{1,0:T(8,128)(2,1)}, bf16[512,2048]{1,0:T(8,128)(2,1)}, bf16[512,2048]{1,0:T(8,128)(2,1)}) custom-call(bf16[512,2048]{1,0:T(8,128)(2,1)} %q_hbm.1, bf16[512,2048]{1,0:T(8,128)(2,1)} %k_hbm.1, bf16[512,2048]{1,0:T(8,128)(2,1)} %v_hbm.1, bf16[512,2048]{1,0:T(8,128)(2,1)} %o_hbm.1, bf16[512,2048]{1,0:T(8,128)(2,1)} %g_hbm.1, ...), custom_call_target="tpu_custom_call" | custom-call | tf_op jit(solution)/shard_map/pallas_call | solution.py:273
  71.2 0.0 copy-start.1
  71.2 3.3 %copy.14 = bf16[512,2048]{1,0:T(8,128)(2,1)} copy(bf16[512,2048]{1,0:T(8,128)(2,1)} %get-tuple-element.6) | data formatting | bytes 4194304
  74.5 0.0 copy-done.1
  74.5 0.0 copy-start
  74.5 1.3 %copy.15 = bf16[512,2048]{1,0:T(8,128)(2,1)} copy(bf16[512,2048]{1,0:T(8,128)(2,1)S(1)} %copy-done.1) | data formatting | bytes 4194304
  75.8 1.0 %copy-done = bf16[512,2048]{1,0:T(8,128)(2,1)S(1)} copy-done((bf16[512,2048]{1,0:T(8,128)(2,1)S(1)}, bf16[512,2048]{1,0:T(8,128)(2,1)}, u32[]{:S(2)}) %copy-start) | copy-done | bytes 2097176
  76.8 1.3 %copy.16 = bf16[512,2048]{1,0:T(8,128)(2,1)} copy(bf16[512,2048]{1,0:T(8,128)(2,1)S(1)} %copy-done) | data formatting | bytes 4194304
Async XLA Ops:
  71.2 3.3 %copy-start.1 = (bf16[512,2048]{1,0:T(8,128)(2,1)S(1)}, bf16[512,2048]{1,0:T(8,128)(2,1)}, u32[]{:S(2)}) copy-start(bf16[512,2048]{1,0:T(8,128)(2,1)} %get-tuple-element.7) | copy-start | bytes 6291460
  74.5 2.3 %copy-start = (bf16[512,2048]{1,0:T(8,128)(2,1)S(1)}, bf16[512,2048]{1,0:T(8,128)(2,1)}, u32[]{:S(2)}) copy-start(bf16[512,2048]{1,0:T(8,128)(2,1)} %get-tuple-element.8) | copy-start | bytes 6291460

commit v2 on v1

v2 whole, which is shorter than its diff:
```python
import functools

import jax
import jax.numpy as jnp
from jax import lax
from jax.experimental import pallas as pl
from jax.experimental.pallas import tpu as pltpu
from jax.sharding import PartitionSpec as P

MESH = pl.DeviceIdType.MESH
LOG2E = 1.4426950408889634
HEAD = 128
LEAD = 2
AHEAD = 3
LAG = 3
HIDDEN = -1e30


def dot(a, b, contract):
    return lax.dot_general(
        a, b, ((contract[:1], contract[1:]), ((), ())), preferred_element_type=jnp.float32
    )


def kernel(
    groups,
    group_size,
    heads,
    q_hbm,
    k_hbm,
    v_hbm,
    o_hbm,
    g_hbm,
    lse_hbm,
    start_hbm,
    window_hbm,
    dq_out,
    dk_out,
    dv_out,
    q_own,
    k_own,
    v_own,
    g_own,
    o_all,
    g_all,
    lse_own,
    start_own,
    window_own,
    stats_own,
    stats_next,
    bias,
    q_next,
    g_next,
    dk_part,
    dv_part,
    dq_own,
    dq_sent,
    dq_got,
    load_sem,
    head_sem,
    send_sem,
    recv_sem,
    stats_sem,
    back_send_sem,
    back_recv_sem,
):
    rows = q_hbm.shape[0]
    half = rows // 2
    count = groups * group_size
    here = lax.axis_index("grp") * group_size + lax.axis_index("seq")
    has_before, has_after = here > 0, here < count - 1
    scale = HEAD**-0.5
    lo, hi = slice(0, half), slice(half, rows)

    def place(index):
        return (index // group_size, lax.rem(index, group_size))

    before = place(lax.rem(here + count - 1, count))
    after = place(lax.rem(here + 1, count))

    def columns(h):
        return pl.ds(pl.multiple_of(h * HEAD, HEAD), HEAD)

    def head_load(h, number):
        source, target = ((q_hbm, q_own), (g_hbm, g_own), (k_hbm, k_own), (v_hbm, v_own))[number]
        return pltpu.make_async_copy(
            source.at[:, columns(h)], target.at[h], head_sem.at[number, h]
        )

    def to_before(h):
        return [
            pltpu.make_async_remote_copy(
                src_ref=source.at[h],
                dst_ref=target.at[h],
                send_sem=send_sem.at[number, h],
                recv_sem=recv_sem.at[number, h],
                device_id=before,
                device_id_type=MESH,
            )
            for number, (source, target) in enumerate(((q_own, q_next), (g_own, g_next)))
        ]

    def to_after(h):
        return pltpu.make_async_remote_copy(
            src_ref=dq_sent.at[h],
            dst_ref=dq_got.at[h],
            send_sem=back_send_sem.at[h],
            recv_sem=back_recv_sem.at[h],
            device_id=after,
            device_id_type=MESH,
        )

    stats_copy = pltpu.make_async_remote_copy(
        src_ref=stats_own,
        dst_ref=stats_next,
        send_sem=stats_sem.at[0],
        recv_sem=stats_sem.at[1],
        device_id=before,
        device_id_type=MESH,
    )

    whole_loads = [
        pltpu.make_async_copy(source, target, load_sem.at[number])
        for number, (source, target) in enumerate(
            (
                (o_hbm, o_all),
                (g_hbm, g_all),
                (lse_hbm, lse_own),
                (start_hbm, start_own),
                (window_hbm, window_own),
            )
        )
    ]
    head_load(0, 0).start()
    head_load(0, 1).start()
    for copy in whole_loads:
        copy.start()

    def start_loads(h, carry):
        for number in range(4):
            if number < 2:

                @pl.when(h > 0)
                def _():
                    head_load(h, number).start()

            else:
                head_load(h, number).start()
        return carry

    lax.fori_loop(0, heads, start_loads, 0)

    barrier = pltpu.get_barrier_semaphore()
    for neighbour in (before, after):
        pl.semaphore_signal(barrier, inc=1, device_id=neighbour, device_id_type=MESH)
    pl.semaphore_wait(barrier, 2)

    def admit(h):
        head_load(h, 0).wait()
        head_load(h, 1).wait()

        @pl.when(has_before)
        def _():
            for copy in to_before(h):
                copy.start()

    admit(0)

    for copy in whole_loads:
        copy.wait()
    positions = lax.broadcasted_iota(jnp.int32, (1, rows), 1)
    lowest = jnp.maximum(
        start_own[...].reshape(1, rows) - here * rows,
        positions - window_own[...].reshape(1, rows) + 1,
    )
    stats_own[0:heads, :] = lse_own[...] * LOG2E
    model = heads * HEAD
    picks = (
        lax.broadcasted_iota(jnp.int32, (heads, model), 1) // HEAD
        == lax.broadcasted_iota(jnp.int32, (heads, model), 0)
    ).astype(jnp.float32).astype(jnp.bfloat16)
    for r in range(0, rows, 128):
        products = o_all[r : r + 128, :].astype(jnp.float32) * g_all[r : r + 128, :].astype(
            jnp.float32
        )
        high = products.astype(jnp.bfloat16)
        low = (products - high.astype(jnp.float32)).astype(jnp.bfloat16)
        stats_own[heads : 2 * heads, r : r + 128] = dot(picks, high, (1, 1)) + dot(
            picks, low, (1, 1)
        )
    stats_own[2 * heads : 2 * heads + 8, :] = jnp.broadcast_to(
        (lowest + rows).astype(jnp.float32), (8, rows)
    )

    @pl.when(has_before)
    def _():
        stats_copy.start()

    for h in range(1, AHEAD):
        admit(h)

    key_at = lax.broadcasted_iota(jnp.int32, (half, half), 0)
    query_at = lax.broadcasted_iota(jnp.int32, (half, half), 1)

    def hidden_where_not(mask):
        return jnp.where(mask, 0.0, HIDDEN)

    bias[0] = hidden_where_not((key_at >= lowest[:, lo]) & (key_at <= query_at))
    bias[1] = hidden_where_not(key_at >= lowest[:, hi])
    bias[2] = hidden_where_not((key_at + half >= lowest[:, hi]) & (key_at <= query_at))

    def pair_block(k, v, q, g, lse, delta, number):
        s = dot(k, q, (1, 1)) * (scale * LOG2E) + bias[number]
        p = jnp.exp2(s - lse)
        ds = p * (dot(v, g, (1, 1)) - delta)
        return p.astype(jnp.bfloat16), ds.astype(jnp.bfloat16)

    def local(h):
        k, v, q, g = k_own[h], v_own[h], q_own[h], g_own[h]
        kt = k.T
        lse = stats_own[pl.ds(h, 1), :]
        delta = stats_own[pl.ds(heads + h, 1), :]

        def block(us, ts, number):
            return pair_block(k[us], v[us], q[ts], g[ts], lse[:, ts], delta[:, ts], number)

        p00, s00 = block(lo, lo, 0)
        p01, s01 = block(lo, hi, 1)
        p11, s11 = block(hi, hi, 2)
        slot = lax.rem(h, LEAD + 1)
        dv_part[slot, lo] = dot(jnp.concatenate([p00, p01], axis=1), g, (1, 0))
        dv_part[slot, hi] = dot(p11, g[hi], (1, 0))
        dk_part[slot, lo] = dot(jnp.concatenate([s00, s01], axis=1), q, (1, 0))
        dk_part[slot, hi] = dot(s11, q[hi], (1, 0))
        dq_own[h, :, lo] = dot(kt[:, lo], s00, (1, 0))
        dq_own[h, :, hi] = dot(kt, jnp.concatenate([s01, s11], axis=0), (1, 0))

    def shared(h):
        k, v, q, g = k_own[h], v_own[h], q_next[h], g_next[h]
        kt = k.T
        lse = stats_next[pl.ds(h, 1), :]
        delta = stats_next[pl.ds(heads + h, 1), :]

        def block(us, ts, number):
            return pair_block(k[us], v[us], q[ts], g[ts], lse[:, ts], delta[:, ts], number)

        p10, s10 = block(hi, lo, 3)
        p00, s00 = block(lo, lo, 4)
        p11, s11 = block(hi, hi, 5)
        dq_sent[h, :, lo] = dot(kt, jnp.concatenate([s00, s10], axis=0), (1, 0)).astype(
            jnp.bfloat16
        )
        dq_sent[h, :, hi] = dot(kt[:, hi], s11, (1, 0)).astype(jnp.bfloat16)
        slot = lax.rem(h, LEAD + 1)
        cols = columns(h)
        dv0 = dv_part[slot, lo] + dot(p00, g[lo], (1, 0))
        dv1 = dv_part[slot, hi] + dot(jnp.concatenate([p10, p11], axis=1), g, (1, 0))
        dk0 = dk_part[slot, lo] + dot(s00, q[lo], (1, 0))
        dk1 = dk_part[slot, hi] + dot(jnp.concatenate([s10, s11], axis=1), q, (1, 0))
        dv_out[lo, cols] = dv0.astype(jnp.bfloat16)
        dv_out[hi, cols] = dv1.astype(jnp.bfloat16)
        dk_out[lo, cols] = (dk0 * scale).astype(jnp.bfloat16)
        dk_out[hi, cols] = (dk1 * scale).astype(jnp.bfloat16)

    def finish(h):
        @pl.when(has_before)
        def _():
            to_after(h).wait_recv()

        total = (dq_own[h] + dq_got[h].astype(jnp.float32)) * scale
        dq_out[:, columns(h)] = total.T.astype(jnp.bfloat16)

    def lead(h, carry):
        head_load(h, 2).wait()
        head_load(h, 3).wait()
        local(h)
        return carry

    lax.fori_loop(0, LEAD, lead, 0)

    @pl.when(has_after)
    def _():
        stats_copy.wait_recv()

    @pl.when(jnp.logical_not(has_after))
    def _():
        stats_next[...] = jnp.full_like(stats_next, 2.0 * rows)

        def clear(h, carry):
            q_next[h] = jnp.zeros((rows, HEAD), jnp.bfloat16)
            g_next[h] = jnp.zeros((rows, HEAD), jnp.bfloat16)
            return carry

        lax.fori_loop(0, heads, clear, 0)

    @pl.when(jnp.logical_not(has_before))
    def _():
        def clear(h, carry):
            dq_got[h] = jnp.zeros((HEAD, rows), jnp.bfloat16)
            return carry

        lax.fori_loop(0, heads, clear, 0)

    bound = stats_next[2 * heads : 2 * heads + 1, :].astype(jnp.int32)
    bias[3] = hidden_where_not(key_at + half >= bound[:, lo])
    bias[4] = hidden_where_not(key_at >= bound[:, lo])
    bias[5] = hidden_where_not(key_at + half >= bound[:, hi])

    def step(h, more):
        if more:

            @pl.when(has_before)
            def _():
                for copy in to_before(h):
                    copy.wait_send()

            @pl.when(h + AHEAD < heads)
            def _():
                admit(h + AHEAD)

            head_load(h + LEAD, 2).wait()
            head_load(h + LEAD, 3).wait()

        @pl.when(has_after)
        def _():
            for copy in to_before(h):
                copy.wait_recv()

        shared(h)
        if more:
            local(h + LEAD)

        @pl.when(has_after)
        def _():
            to_after(h).start()

        @pl.when(h >= LAG)
        def _():
            finish(h - LAG)

    def both(h, carry):
        step(h, True)
        return carry

    def shared_only(h, carry):
        step(h, False)
        return carry

    lax.fori_loop(0, heads - LEAD, both, 0)
    lax.fori_loop(heads - LEAD, heads, shared_only, 0)
    lax.fori_loop(heads - LAG, heads, lambda h, c: (finish(h), c)[1], 0)

    def drain(h, carry):
        @pl.when(has_after)
        def _():
            to_after(h).wait_send()

        @pl.when(has_before & (h >= heads - LEAD))
        def _():
            for copy in to_before(h):
                copy.wait_send()

        return carry

    lax.fori_loop(0, heads, drain, 0)

    @pl.when(has_before)
    def _():
        stats_copy.wait_send()


def solution(mesh):
    groups, group_size = mesh.shape["grp"], mesh.shape["seq"]

    def local(q, k, v, o, g, lse, start, window):
        rows, model = q.shape
        heads = lse.shape[0]
        block = pltpu.VMEM((rows, model), jnp.bfloat16)
        per_head = pltpu.VMEM((heads, rows, HEAD), jnp.bfloat16)
        turned = pltpu.VMEM((heads, HEAD, rows), jnp.bfloat16)
        stats = pltpu.VMEM((2 * heads + 8, rows), jnp.float32)
        part = pltpu.VMEM((LEAD + 1, rows, HEAD), jnp.float32)
        return pl.pallas_call(
            functools.partial(kernel, groups, group_size, heads),
            out_shape=(block, block, block),
            in_specs=[pl.BlockSpec(memory_space=pl.ANY)] * 8,
            out_specs=(pl.BlockSpec(memory_space=pltpu.VMEM),) * 3,
            scratch_shapes=[
                per_head,
                per_head,
                per_head,
                per_head,
                block,
                block,
                pltpu.VMEM((heads, rows), jnp.float32),
                pltpu.VMEM((rows,), jnp.int32),
                pltpu.VMEM((rows,), jnp.int32),
                stats,
                stats,
                pltpu.VMEM((6, rows // 2, rows // 2), jnp.float32),
                per_head,
                per_head,
                part,
                part,
                pltpu.VMEM((heads, HEAD, rows), jnp.float32),
                turned,
                turned,
                pltpu.SemaphoreType.DMA((5,)),
                pltpu.SemaphoreType.DMA((4, heads)),
                pltpu.SemaphoreType.DMA((2, heads)),
                pltpu.SemaphoreType.DMA((2, heads)),
                pltpu.SemaphoreType.DMA((2,)),
                pltpu.SemaphoreType.DMA((heads,)),
                pltpu.SemaphoreType.DMA((heads,)),
            ],
            compiler_params=pltpu.CompilerParams(
                collective_id=0, has_side_effects=True, vmem_limit_bytes=48 * 2**20
            ),
        )(q, k, v, o, g, lse, start, window)

    block = P(("grp", "seq"), None)
    return jax.shard_map(
        local,
        mesh=mesh,
        in_specs=(block,) * 5 + (P(None, ("grp", "seq")),) + (P(("grp", "seq")),) * 2,
        out_specs=(block,) * 3,
        check_vma=False,
    )
```

time: 78.3 us -> 69.4 us (0.89)
  the two profiles are of different devices: /device:TPU:0 before, /device:TPU:6 now
where the time goes in v2:
time: 69.4 us; the launch traced here: 69.3 us
  Pallas kernels  64.7 us (93%)
  local copies, waits for them, and re-layouts  3.96 us (6%)
    pallas_call x1, Pallas kernels, local(): pl.pallas_call(functools.partial(kernel, groups, group_size, heads), out_...  64.7 us
    unnamed x3, local copies, waits for them, and re-layouts  3.96 us

profile of v2, /device:TPU:6, one launch (start us, length us, event | category | flops | bytes accessed | tf_op | source)
XLA Modules:
  0.0 69.3 jit_solution(10791918475150119037)
XLA Ops:
  0.6 64.7 %shard_map.103 = (bf16[512,2048]{1,0:T(8,128)(2,1)S(1)}, bf16[512,2048]{1,0:T(8,128)(2,1)S(1)}, bf16[512,2048]{1,0:T(8,128)(2,1)S(1)}) custom-call(bf16[512,2048]{1,0:T(8,128)(2,1)} %q_hbm.1, bf16[512,2048]{1,0:T(8,128)(2,1)} %k_hbm.1, bf16[512,2048]{1,0:T(8,128)(2,1)} %v_hbm.1, bf16[512,2048]{1,0:T(8,128)(2,1)} %o_hbm.1, bf16[512,2048]{1,0:T(8,128)(2,1)} %g_hbm.1, ...), custom_call_target="tpu_custom_call" | custom-call | tf_op jit(solution)/shard_map/pallas_call | solution.py:383
  65.3 1.3 %copy.14 = bf16[512,2048]{1,0:T(8,128)(2,1)} copy(bf16[512,2048]{1,0:T(8,128)(2,1)S(1)} %get-tuple-element.3) | data formatting | bytes 4194304
  66.6 1.3 %copy.15 = bf16[512,2048]{1,0:T(8,128)(2,1)} copy(bf16[512,2048]{1,0:T(8,128)(2,1)S(1)} %get-tuple-element.4) | data formatting | bytes 4194304
  68.0 1.3 %copy.16 = bf16[512,2048]{1,0:T(8,128)(2,1)} copy(bf16[512,2048]{1,0:T(8,128)(2,1)S(1)} %get-tuple-element.5) | data formatting | bytes 4194304

commit v3 on v2

--- a/solution.py
+++ b/solution.py
@@ -13,6 +13,7 @@
 LEAD = 2
 AHEAD = 3
 LAG = 3
+TURNED = 3
 HIDDEN = -1e30
 
 
@@ -56,6 +57,12 @@
     dq_own,
     dq_sent,
     dq_got,
+    k_before,
+    v_before,
+    dk_sent,
+    dv_sent,
+    dk_got,
+    dv_got,
     load_sem,
     head_sem,
     send_sem,
@@ -63,6 +70,10 @@
     stats_sem,
     back_send_sem,
     back_recv_sem,
+    keys_send_sem,
+    keys_recv_sem,
+    grads_send_sem,
+    grads_recv_sem,
 ):
     rows = q_hbm.shape[0]
     half = rows // 2
@@ -110,6 +121,32 @@
             device_id_type=MESH,
         )
 
+    def keys_to_after(h):
+        return [
+            pltpu.make_async_remote_copy(
+                src_ref=source.at[h],
+                dst_ref=target.at[h],
+                send_sem=keys_send_sem.at[number, h],
+                recv_sem=keys_recv_sem.at[number, h],
+                device_id=after,
+                device_id_type=MESH,
+            )
+            for number, (source, target) in enumerate(((k_own, k_before), (v_own, v_before)))
+        ]
+
+    def grads_to_before(h):
+        return [
+            pltpu.make_async_remote_copy(
+                src_ref=source.at[h],
+                dst_ref=target.at[h],
+                send_sem=grads_send_sem.at[number, h],
+                recv_sem=grads_recv_sem.at[number, h],
+                device_id=before,
+                device_id_type=MESH,
+            )
+            for number, (source, target) in enumerate(((dk_sent, dk_got), (dv_sent, dv_got)))
+        ]
+
     stats_copy = pltpu.make_async_remote_copy(
         src_ref=stats_own,
         dst_ref=stats_next,
@@ -131,28 +168,29 @@
             )
         )
     ]
-    head_load(0, 0).start()
-    head_load(0, 1).start()
-    for copy in whole_loads:
-        copy.start()
-
-    def start_loads(h, carry):
-        for number in range(4):
-            if number < 2:
-
-                @pl.when(h > 0)
-                def _():
-                    head_load(h, number).start()
-
-            else:
-                head_load(h, number).start()
-        return carry
-
-    lax.fori_loop(0, heads, start_loads, 0)
-
     barrier = pltpu.get_barrier_semaphore()
     for neighbour in (before, after):
         pl.semaphore_signal(barrier, inc=1, device_id=neighbour, device_id_type=MESH)
+
+    head_load(TURNED, 0).start()
+    head_load(TURNED, 1).start()
+    for h in range(TURNED):
+        head_load(h, 2).start()
+        head_load(h, 3).start()
+    for copy in whole_loads:
+        copy.start()
+
+    def start_loads(h, carry):
+        for number in range(4):
+            first = (h != TURNED) if number < 2 else (h >= TURNED)
+
+            @pl.when(first)
+            def _():
+                head_load(h, number).start()
+
+        return carry
+
+    lax.fori_loop(0, heads, start_loads, 0)
     pl.semaphore_wait(barrier, 2)
 
     def admit(h):
@@ -164,7 +202,16 @@
             for copy in to_before(h):
                 copy.start()
 
-    admit(0)
+    admit(TURNED)
+    for h in range(TURNED):
+        head_load(h, 2).wait()
+        head_load(h, 3).wait()
+
+        @pl.when(has_after)
+        def _():
+            for copy in keys_to_after(h):
+                copy.start()
+
 
     for copy in whole_loads:
         copy.wait()
@@ -196,8 +243,11 @@
     def _():
         stats_copy.start()
 
-    for h in range(1, AHEAD):
+    for h in range(TURNED + 1, TURNED + AHEAD):
         admit(h)
+    for h in range(TURNED):
+        head_load(h, 0).wait()
+        head_load(h, 1).wait()
 
     key_at = lax.broadcasted_iota(jnp.int32, (half, half), 0)
     query_at = lax.broadcasted_iota(jnp.int32, (half, half), 1)
@@ -208,6 +258,10 @@
     bias[0] = hidden_where_not((key_at >= lowest[:, lo]) & (key_at <= query_at))
     bias[1] = hidden_where_not(key_at >= lowest[:, hi])
     bias[2] = hidden_where_not((key_at + half >= lowest[:, hi]) & (key_at <= query_at))
+
+    bias[6] = hidden_where_not(key_at - half >= lowest[:, lo])
+    bias[7] = hidden_where_not(key_at - rows >= lowest[:, lo])
+    bias[8] = hidden_where_not(key_at - half >= lowest[:, hi])
 
     def pair_block(k, v, q, g, lse, delta, number):
         s = dot(k, q, (1, 1)) * (scale * LOG2E) + bias[number]
@@ -227,7 +281,7 @@
         p00, s00 = block(lo, lo, 0)
         p01, s01 = block(lo, hi, 1)
         p11, s11 = block(hi, hi, 2)
-        slot = lax.rem(h, LEAD + 1)
+        slot = h
         dv_part[slot, lo] = dot(jnp.concatenate([p00, p01], axis=1), g, (1, 0))
         dv_part[slot, hi] = dot(p11, g[hi], (1, 0))
         dk_part[slot, lo] = dot(jnp.concatenate([s00, s01], axis=1), q, (1, 0))
@@ -251,7 +305,7 @@
             jnp.bfloat16
         )
         dq_sent[h, :, hi] = dot(kt[:, hi], s11, (1, 0)).astype(jnp.bfloat16)
-        slot = lax.rem(h, LEAD + 1)
+        slot = h
         cols = columns(h)
         dv0 = dv_part[slot, lo] + dot(p00, g[lo], (1, 0))
         dv1 = dv_part[slot, hi] + dot(jnp.concatenate([p10, p11], axis=1), g, (1, 0))
@@ -262,6 +316,42 @@
         dk_out[lo, cols] = (dk0 * scale).astype(jnp.bfloat16)
         dk_out[hi, cols] = (dk1 * scale).astype(jnp.bfloat16)
 
+    def turned(h):
+        for copy in keys_to_after(h):
+            copy.wait_recv()
+        k, v, q, g = k_before[h], v_before[h], q_own[h], g_own[h]
+        kt = k.T
+        lse = stats_own[pl.ds(h, 1), :]
+        delta = stats_own[pl.ds(heads + h, 1), :]
+
+        def block(us, ts, number):
+            return pair_block(k[us], v[us], q[ts], g[ts], lse[:, ts], delta[:, ts], number)
+
+        p10, s10 = block(hi, lo, 6)
+        p00, s00 = block(lo, lo, 7)
+        p11, s11 = block(hi, hi, 8)
+        dq_own[h, :, lo] += dot(kt, jnp.concatenate([s00, s10], axis=0), (1, 0))
+        dq_own[h, :, hi] += dot(kt[:, hi], s11, (1, 0))
+        dv0 = dot(p00, g[lo], (1, 0))
+        dv1 = dot(jnp.concatenate([p10, p11], axis=1), g, (1, 0))
+        dk0 = dot(s00, q[lo], (1, 0))
+        dk1 = dot(jnp.concatenate([s10, s11], axis=1), q, (1, 0))
+        dv_sent[h, lo] = dv0.astype(jnp.bfloat16)
+        dv_sent[h, hi] = dv1.astype(jnp.bfloat16)
+        dk_sent[h, lo] = dk0.astype(jnp.bfloat16)
+        dk_sent[h, hi] = dk1.astype(jnp.bfloat16)
+
+    def finish_turned(h):
+        @pl.when(has_after)
+        def _():
+            for copy in grads_to_before(h):
+                copy.wait_recv()
+            dk_part[h] += dk_got[h].astype(jnp.float32)
+            dv_part[h] += dv_got[h].astype(jnp.float32)
+
+        dk_out[:, columns(h)] = (dk_part[h] * scale).astype(jnp.bfloat16)
+        dv_out[:, columns(h)] = dv_part[h].astype(jnp.bfloat16)
+
     def finish(h):
         @pl.when(has_before)
         def _():
@@ -271,12 +361,15 @@
         dq_out[:, columns(h)] = total.T.astype(jnp.bfloat16)
 
     def lead(h, carry):
-        head_load(h, 2).wait()
-        head_load(h, 3).wait()
+        @pl.when(h >= TURNED)
+        def _():
+            head_load(h, 2).wait()
+            head_load(h, 3).wait()
+
         local(h)
         return carry
 
-    lax.fori_loop(0, LEAD, lead, 0)
+    lax.fori_loop(0, TURNED + LEAD, lead, 0)
 
     @pl.when(has_after)
     def _():
@@ -318,6 +411,19 @@
             def _():
                 admit(h + AHEAD)
 
+        else:
+
+            @pl.when(has_before)
+            def _():
+                for copy in to_before(h):
+                    copy.wait_send()
+
+        @pl.when(has_before & (h + AHEAD >= heads))
+        def _():
+            for copy in grads_to_before(h + AHEAD - heads):
+                copy.start()
+
+        if more:
             head_load(h + LEAD, 2).wait()
             head_load(h + LEAD, 3).wait()
 
@@ -334,7 +440,17 @@
         def _():
             to_after(h).start()
 
-        @pl.when(h >= LAG)
+        @pl.when((h > TURNED) & (h <= 2 * TURNED))
+        def _():
+            @pl.when(has_before)
+            def _():
+                turned(h - TURNED - 1)
+
+            dq_out[:, columns(h - TURNED - 1)] = (
+                (dq_own[h - TURNED - 1] * scale).T.astype(jnp.bfloat16)
+            )
+
+        @pl.when(h >= TURNED + LAG)
         def _():
             finish(h - LAG)
 
@@ -346,18 +462,24 @@
         step(h, False)
         return carry
 
-    lax.fori_loop(0, heads - LEAD, both, 0)
+    lax.fori_loop(TURNED, heads - LEAD, both, 0)
     lax.fori_loop(heads - LEAD, heads, shared_only, 0)
     lax.fori_loop(heads - LAG, heads, lambda h, c: (finish(h), c)[1], 0)
+    lax.fori_loop(0, TURNED, lambda h, c: (finish_turned(h), c)[1], 0)
 
     def drain(h, carry):
-        @pl.when(has_after)
+        @pl.when(has_after & (h >= TURNED))
         def _():
             to_after(h).wait_send()
 
-        @pl.when(has_before & (h >= heads - LEAD))
-        def _():
-            for copy in to_before(h):
+        @pl.when(has_after & (h < TURNED))
+        def _():
+            for copy in keys_to_after(h):
+                copy.wait_send()
+
+        @pl.when(has_before & (h < TURNED))
+        def _():
+            for copy in grads_to_before(h):
                 copy.wait_send()
 
         return carry
@@ -367,6 +489,18 @@
     @pl.when(has_before)
     def _():
         stats_copy.wait_send()
+
+
+def write_out(*refs):
+    sources, targets, sem = refs[:3], refs[3:6], refs[6]
+    copies = [
+        pltpu.make_async_copy(source, target, sem.at[number])
+        for number, (source, target) in enumerate(zip(sources, targets))
+    ]
+    for copy in copies:
+        copy.start()
+    for copy in copies:
+        copy.wait()
 
 
 def solution(mesh):
@@ -379,8 +513,9 @@
         per_head = pltpu.VMEM((heads, rows, HEAD), jnp.bfloat16)
         turned = pltpu.VMEM((heads, HEAD, rows), jnp.bfloat16)
         stats = pltpu.VMEM((2 * heads + 8, rows), jnp.float32)
-        part = pltpu.VMEM((LEAD + 1, rows, HEAD), jnp.float32)
-        return pl.pallas_call(
+        part = pltpu.VMEM((heads, rows, HEAD), jnp.float32)
+        few = pltpu.VMEM((TURNED, rows, HEAD), jnp.bfloat16)
+        results = pl.pallas_call(
             functools.partial(kernel, groups, group_size, heads),
             out_shape=(block, block, block),
             in_specs=[pl.BlockSpec(memory_space=pl.ANY)] * 8,
@@ -397,7 +532,7 @@
                 pltpu.VMEM((rows,), jnp.int32),
                 stats,
                 stats,
-                pltpu.VMEM((6, rows // 2, rows // 2), jnp.float32),
+                pltpu.VMEM((9, rows // 2, rows // 2), jnp.float32),
                 per_head,
                 per_head,
                 part,
@@ -405,6 +540,12 @@
                 pltpu.VMEM((heads, HEAD, rows), jnp.float32),
                 turned,
                 turned,
+                few,
+                few,
+                few,
+                few,
+                few,
+                few,
                 pltpu.SemaphoreType.DMA((5,)),
                 pltpu.SemaphoreType.DMA((4, heads)),
                 pltpu.SemaphoreType.DMA((2, heads)),
@@ -412,11 +553,23 @@
                 pltpu.SemaphoreType.DMA((2,)),
                 pltpu.SemaphoreType.DMA((heads,)),
                 pltpu.SemaphoreType.DMA((heads,)),
+                pltpu.SemaphoreType.DMA((2, TURNED)),
+                pltpu.SemaphoreType.DMA((2, TURNED)),
+                pltpu.SemaphoreType.DMA((2, TURNED)),
+                pltpu.SemaphoreType.DMA((2, TURNED)),
             ],
             compiler_params=pltpu.CompilerParams(
                 collective_id=0, has_side_effects=True, vmem_limit_bytes=48 * 2**20
             ),
         )(q, k, v, o, g, lse, start, window)
+        return pl.pallas_call(
+            write_out,
+            out_shape=(jax.ShapeDtypeStruct((rows, model), jnp.bfloat16),) * 3,
+            in_specs=[pl.BlockSpec(memory_space=pltpu.VMEM)] * 3,
+            out_specs=(pl.BlockSpec(memory_space=pl.ANY),) * 3,
+            scratch_shapes=[pltpu.SemaphoreType.DMA((3,))],
+            compiler_params=pltpu.CompilerParams(vmem_limit_bytes=8 * 2**20),
+        )(*(pltpu.with_memory_space_constraint(r, pltpu.VMEM) for r in results))
 
     block = P(("grp", "seq"), None)
     return jax.shard_map(

time: 69.4 us -> 60.1 us (0.87)
  Pallas kernels: 64.7 us -> 59.4 us
  local copies, waits for them, and re-layouts: 3.96 us -> 0 us
    pallas_call x1, Pallas kernels: 64.7 us -> 56.7 us  [local(): pl.pallas_call(functools.partial(kernel, groups, group_size, heads), out_...]
    unnamed x3 -> x0, local copies, waits for them, and re-layouts: 3.96 us -> none
    pallas_call x0 -> x1, Pallas kernels: none -> 2.73 us  [local(): pl.pallas_call(write_out, out_shape=(jax.ShapeDtypeStruct((rows, model),...]
where the time goes in v3:
time: 60.1 us; the launch traced here: 60 us
  Pallas kernels  59.4 us (99%)
  between operations  0.64 us (1%)
    pallas_call x1, Pallas kernels, local(): pl.pallas_call(functools.partial(kernel, groups, group_size, heads), out_...  56.7 us
    pallas_call x1, Pallas kernels, local(): pl.pallas_call(write_out, out_shape=(jax.ShapeDtypeStruct((rows, model),...  2.73 us

profile of v3, /device:TPU:6, one launch (start us, length us, event | category | flops | bytes accessed | tf_op | source)
XLA Modules:
  0.0 60.0 jit_solution(3983601750068966826)
XLA Ops:
  0.6 56.7 %shard_map.103 = (bf16[512,2048]{1,0:T(8,128)(2,1)S(1)}, bf16[512,2048]{1,0:T(8,128)(2,1)S(1)}, bf16[512,2048]{1,0:T(8,128)(2,1)S(1)}) custom-call(bf16[512,2048]{1,0:T(8,128)(2,1)} %q_hbm.1, bf16[512,2048]{1,0:T(8,128)(2,1)} %k_hbm.1, bf16[512,2048]{1,0:T(8,128)(2,1)} %v_hbm.1, bf16[512,2048]{1,0:T(8,128)(2,1)} %o_hbm.1, bf16[512,2048]{1,0:T(8,128)(2,1)} %g_hbm.1, ...), custom_call_target="tpu_custom_call" | custom-call | tf_op jit(solution)/shard_map/pallas_call | solution.py:518
  57.3 2.7 %shard_map.104 = (bf16[512,2048]{1,0:T(8,128)(2,1)}, bf16[512,2048]{1,0:T(8,128)(2,1)}, bf16[512,2048]{1,0:T(8,128)(2,1)}) custom-call(bf16[512,2048]{1,0:T(8,128)(2,1)S(1)} %get-tuple-element.6.refs_0_, bf16[512,2048]{1,0:T(8,128)(2,1)S(1)} %get-tuple-element.7.refs_1_, bf16[512,2048]{1,0:T(8,128)(2,1)S(1)} %get-tuple-element.8.refs_2_), custom_call_target="tpu_custom_call" | custom-call | tf_op jit(solution)/shard_map/pallas_call | solution.py:565

commit v4 on v3

--- a/solution.py
+++ b/solution.py
@@ -12,8 +12,13 @@
 HEAD = 128
 LEAD = 2
 AHEAD = 3
-LAG = 3
+LAG = 5
 TURNED = 3
+WRAPPED = 3
+PLAIN = 1
+FIRST = 5
+LATE = 2
+EARLY = 2
 HIDDEN = -1e30
 
 
@@ -63,6 +68,8 @@
     dv_sent,
     dk_got,
     dv_got,
+    q_relay,
+    g_relay,
     load_sem,
     head_sem,
     send_sem,
@@ -74,6 +81,10 @@
     keys_recv_sem,
     grads_send_sem,
     grads_recv_sem,
+    relay_send_sem,
+    relay_recv_sem,
+    forward_send_sem,
+    ready_sem,
 ):
     rows = q_hbm.shape[0]
     half = rows // 2
@@ -88,6 +99,24 @@
 
     before = place(lax.rem(here + count - 1, count))
     after = place(lax.rem(here + 1, count))
+
+    core = lax.rem(here, 2)
+    z = lax.rem(here // 2, 4)
+    ring = here - 2 * z - core
+    even_z = lax.rem(z, 2) == 0
+    detours = (core == 0) & has_before
+    detoured = jnp.where(detours, jnp.where(z == 0, WRAPPED, PLAIN), 0)
+    direct = heads - TURNED - detoured
+    leaves = heads - LATE
+    relay_of_here = place(ring + 2 * lax.rem(z + jnp.where(even_z, 2, 1), 4) + 1)
+    relays = (core == 1) & even_z
+    first_client = ring + 2 * lax.rem(z + 2, 4)
+    second_client = ring + 2 * lax.rem(z + 3, 4)
+    relays_first = relays & (first_client > 0)
+    first_count = jnp.where(z == 2, WRAPPED, PLAIN)
+    next_z = lax.rem(z + 1, 4)
+    next_ring = here + 1 - 2 * next_z
+    relay_of_after = place(next_ring + 2 * lax.rem(next_z + jnp.where(even_z, 1, 2), 4) + 1)
 
     def columns(h):
         return pl.ds(pl.multiple_of(h * HEAD, HEAD), HEAD)
@@ -145,6 +174,52 @@
                 device_id_type=MESH,
             )
             for number, (source, target) in enumerate(((dk_sent, dk_got), (dv_sent, dv_got)))
+        ]
+
+    def to_relay(h):
+        slot = h - (leaves - detoured) + jnp.where(even_z, 0, WRAPPED)
+        return [
+            pltpu.make_async_remote_copy(
+                src_ref=source.at[h],
+                dst_ref=target.at[slot],
+                send_sem=relay_send_sem.at[number, slot],
+                recv_sem=relay_recv_sem.at[number, slot],
+                device_id=relay_of_here,
+                device_id_type=MESH,
+            )
+            for number, (source, target) in enumerate(((q_own, q_relay), (g_own, g_relay)))
+        ]
+
+    def forward(slot, h, client):
+        return [
+            pltpu.make_async_remote_copy(
+                src_ref=source.at[slot],
+                dst_ref=target.at[h],
+                send_sem=forward_send_sem.at[number, slot],
+                recv_sem=recv_sem.at[number, h],
+                device_id=place(client - 1),
+                device_id_type=MESH,
+            )
+            for number, (source, target) in enumerate(((q_relay, q_next), (g_relay, g_next)))
+        ]
+
+    def forwards(slot):
+        if slot < WRAPPED:
+            wanted = relays_first & (slot < first_count)
+            return wanted, forward(slot, leaves - first_count + slot, first_client)
+        return relays, forward(slot, leaves - PLAIN + slot - WRAPPED, second_client)
+
+    def arrived(slot):
+        return [
+            pltpu.make_async_remote_copy(
+                src_ref=source.at[0],
+                dst_ref=target.at[slot],
+                send_sem=relay_send_sem.at[number, slot],
+                recv_sem=relay_recv_sem.at[number, slot],
+                device_id=before,
+                device_id_type=MESH,
+            )
+            for number, (source, target) in enumerate(((q_own, q_relay), (g_own, g_relay)))
         ]
 
     stats_copy = pltpu.make_async_remote_copy(
@@ -169,11 +244,20 @@
         )
     ]
     barrier = pltpu.get_barrier_semaphore()
-    for neighbour in (before, after):
-        pl.semaphore_signal(barrier, inc=1, device_id=neighbour, device_id_type=MESH)
-
-    head_load(TURNED, 0).start()
-    head_load(TURNED, 1).start()
+
+    def greet(wanted, device):
+        @pl.when(wanted)
+        def _():
+            pl.semaphore_signal(barrier, inc=1, device_id=device, device_id_type=MESH)
+
+    greet(has_after, after)
+    greet(has_before, before)
+    greet(detours, relay_of_here)
+    greet((core == 1) & has_after, relay_of_after)
+
+    for h in range(TURNED, TURNED + EARLY):
+        head_load(h, 0).start()
+        head_load(h, 1).start()
     for h in range(TURNED):
         head_load(h, 2).start()
         head_load(h, 3).start()
@@ -182,7 +266,7 @@
 
     def start_loads(h, carry):
         for number in range(4):
-            first = (h != TURNED) if number < 2 else (h >= TURNED)
+            first = ((h < TURNED) | (h >= TURNED + EARLY)) if number < 2 else (h >= TURNED)
 
             @pl.when(first)
             def _():
@@ -191,18 +275,40 @@
         return carry
 
     lax.fori_loop(0, heads, start_loads, 0)
-    pl.semaphore_wait(barrier, 2)
+    pl.semaphore_wait(
+        barrier,
+        has_before.astype(jnp.int32)
+        + has_after.astype(jnp.int32)
+        + 2 * relays.astype(jnp.int32)
+        + 2 * relays_first.astype(jnp.int32),
+    )
+
+    @pl.when(relays_first)
+    def _():
+        pl.semaphore_signal(
+            ready_sem, inc=1, device_id=place(first_client), device_id_type=MESH
+        )
+
+    @pl.when(relays)
+    def _():
+        pl.semaphore_signal(
+            ready_sem, inc=1, device_id=place(second_client), device_id_type=MESH
+        )
+
+    def direct_head(item):
+        h = TURNED + item
+        return jnp.where(h < leaves - detoured, h, h + detoured)
 
     def admit(h):
+        @pl.when(has_before)
+        def _():
+            for copy in to_before(h):
+                copy.start()
+
+    for h in range(TURNED, TURNED + EARLY):
         head_load(h, 0).wait()
         head_load(h, 1).wait()
-
-        @pl.when(has_before)
-        def _():
-            for copy in to_before(h):
-                copy.start()
-
-    admit(TURNED)
+        admit(h)
     for h in range(TURNED):
         head_load(h, 2).wait()
         head_load(h, 3).wait()
@@ -243,11 +349,19 @@
     def _():
         stats_copy.start()
 
-    for h in range(TURNED + 1, TURNED + AHEAD):
+    def settle(h, carry):
+        for number in range(4):
+            waits = ((h < TURNED) | (h >= TURNED + EARLY)) if number < 2 else (h >= TURNED)
+
+            @pl.when(waits)
+            def _():
+                head_load(h, number).wait()
+
+        return carry
+
+    lax.fori_loop(0, heads, settle, 0)
+    for h in range(TURNED + EARLY, TURNED + AHEAD):
         admit(h)
-    for h in range(TURNED):
-        head_load(h, 0).wait()
-        head_load(h, 1).wait()
 
     key_at = lax.broadcasted_iota(jnp.int32, (half, half), 0)
     query_at = lax.broadcasted_iota(jnp.int32, (half, half), 1)
@@ -361,15 +475,22 @@
         dq_out[:, columns(h)] = total.T.astype(jnp.bfloat16)
 
     def lead(h, carry):
-        @pl.when(h >= TURNED)
-        def _():
-            head_load(h, 2).wait()
-            head_load(h, 3).wait()
-
         local(h)
         return carry
 
     lax.fori_loop(0, TURNED + LEAD, lead, 0)
+
+    @pl.when(detours)
+    def _():
+        pl.semaphore_wait(ready_sem, 1)
+
+        def leave(h, carry):
+            for copy in to_relay(h):
+                copy.start()
+            return carry
+
+        lax.fori_loop(leaves - detoured, leaves, leave, 0)
+
 
     @pl.when(has_after)
     def _():
@@ -400,32 +521,31 @@
     bias[5] = hidden_where_not(key_at + half >= bound[:, hi])
 
     def step(h, more):
-        if more:
-
-            @pl.when(has_before)
+        item = h - TURNED
+
+        @pl.when(has_before & (item < direct))
+        def _():
+            for copy in to_before(direct_head(item)):
+                copy.wait_send()
+
+        @pl.when(item + AHEAD < direct)
+        def _():
+            admit(direct_head(item + AHEAD))
+
+        @pl.when(has_before & (item + AHEAD >= direct) & (item + AHEAD < direct + TURNED))
+        def _():
+            for copy in grads_to_before(item + AHEAD - direct):
+                copy.start()
+
+        for slot in range(WRAPPED + PLAIN):
+            wanted, copies = forwards(slot)
+
+            @pl.when(wanted & (h == TURNED + FIRST + (slot + PLAIN) % (WRAPPED + PLAIN)))
             def _():
-                for copy in to_before(h):
-                    copy.wait_send()
-
-            @pl.when(h + AHEAD < heads)
-            def _():
-                admit(h + AHEAD)
-
-        else:
-
-            @pl.when(has_before)
-            def _():
-                for copy in to_before(h):
-                    copy.wait_send()
-
-        @pl.when(has_before & (h + AHEAD >= heads))
-        def _():
-            for copy in grads_to_before(h + AHEAD - heads):
-                copy.start()
-
-        if more:
-            head_load(h + LEAD, 2).wait()
-            head_load(h + LEAD, 3).wait()
+                for copy in arrived(slot):
+                    copy.wait_recv()
+                for copy in copies:
+                    copy.start()
 
         @pl.when(has_after)
         def _():
@@ -485,6 +605,23 @@
         return carry
 
     lax.fori_loop(0, heads, drain, 0)
+
+    @pl.when(detours)
+    def _():
+        def left(h, carry):
+            for copy in to_relay(h):
+                copy.wait_send()
+            return carry
+
+        lax.fori_loop(leaves - detoured, leaves, left, 0)
+
+    for slot in range(WRAPPED + PLAIN):
+        wanted, copies = forwards(slot)
+
+        @pl.when(wanted)
+        def _():
+            for copy in copies:
+                copy.wait_send()
 
     @pl.when(has_before)
     def _():
@@ -515,6 +652,7 @@
         stats = pltpu.VMEM((2 * heads + 8, rows), jnp.float32)
         part = pltpu.VMEM((heads, rows, HEAD), jnp.float32)
         few = pltpu.VMEM((TURNED, rows, HEAD), jnp.bfloat16)
+        relay = pltpu.VMEM((WRAPPED + PLAIN, rows, HEAD), jnp.bfloat16)
         results = pl.pallas_call(
             functools.partial(kernel, groups, group_size, heads),
             out_shape=(block, block, block),
@@ -546,6 +684,8 @@
                 few,
                 few,
                 few,
+                relay,
+                relay,
                 pltpu.SemaphoreType.DMA((5,)),
                 pltpu.SemaphoreType.DMA((4, heads)),
                 pltpu.SemaphoreType.DMA((2, heads)),
@@ -557,6 +697,10 @@
                 pltpu.SemaphoreType.DMA((2, TURNED)),
                 pltpu.SemaphoreType.DMA((2, TURNED)),
                 pltpu.SemaphoreType.DMA((2, TURNED)),
+                pltpu.SemaphoreType.DMA((2, WRAPPED + PLAIN)),
+                pltpu.SemaphoreType.DMA((2, WRAPPED + PLAIN)),
+                pltpu.SemaphoreType.DMA((2, WRAPPED + PLAIN)),
+                pltpu.SemaphoreType.REGULAR,
             ],
             compiler_params=pltpu.CompilerParams(
                 collective_id=0, has_side_effects=True, vmem_limit_bytes=48 * 2**20

time: 60.1 us -> 54.2 us (0.902)
  Pallas kernels: 59.4 us -> 53.5 us
    pallas_call x1, Pallas kernels: 56.7 us -> 50.7 us  [local(): pl.pallas_call(functools.partial(kernel, groups, group_size, heads), out_...]
where the time goes in v4:
time: 54.2 us; the launch traced here: 54.1 us
  Pallas kernels  53.5 us (99%)
  between operations  0.64 us (1%)
    pallas_call x1, Pallas kernels, local(): pl.pallas_call(functools.partial(kernel, groups, group_size, heads), out_...  50.7 us
    pallas_call x1, Pallas kernels, local(): pl.pallas_call(write_out, out_shape=(jax.ShapeDtypeStruct((rows, model),...  2.73 us

profile of v4, /device:TPU:6, one launch (start us, length us, event | category | flops | bytes accessed | tf_op | source)
XLA Modules:
  0.0 54.1 jit_solution(9568932738949268180)
XLA Ops:
  0.6 50.7 %shard_map.103 = (bf16[512,2048]{1,0:T(8,128)(2,1)S(1)}, bf16[512,2048]{1,0:T(8,128)(2,1)S(1)}, bf16[512,2048]{1,0:T(8,128)(2,1)S(1)}) custom-call(bf16[512,2048]{1,0:T(8,128)(2,1)} %q_hbm.1, bf16[512,2048]{1,0:T(8,128)(2,1)} %k_hbm.1, bf16[512,2048]{1,0:T(8,128)(2,1)} %v_hbm.1, bf16[512,2048]{1,0:T(8,128)(2,1)} %o_hbm.1, bf16[512,2048]{1,0:T(8,128)(2,1)} %g_hbm.1, ...), custom_call_target="tpu_custom_call" | custom-call | tf_op jit(solution)/shard_map/pallas_call | solution.py:656
  51.4 2.7 %shard_map.104 = (bf16[512,2048]{1,0:T(8,128)(2,1)}, bf16[512,2048]{1,0:T(8,128)(2,1)}, bf16[512,2048]{1,0:T(8,128)(2,1)}) custom-call(bf16[512,2048]{1,0:T(8,128)(2,1)S(1)} %get-tuple-element.6.refs_0_, bf16[512,2048]{1,0:T(8,128)(2,1)S(1)} %get-tuple-element.7.refs_1_, bf16[512,2048]{1,0:T(8,128)(2,1)S(1)} %get-tuple-element.8.refs_2_), custom_call_target="tpu_custom_call" | custom-call | tf_op jit(solution)/shard_map/pallas_call | solution.py:709

commit v5 on v4

--- a/solution.py
+++ b/solution.py
@@ -11,14 +11,15 @@
 LOG2E = 1.4426950408889634
 HEAD = 128
 LEAD = 2
-AHEAD = 3
-LAG = 5
+AHEAD = 4
+LAG = 9
 TURNED = 3
 WRAPPED = 3
 PLAIN = 1
-FIRST = 5
+PACE = 2
+FORWARDED = (4, 6, 8, 2)
 LATE = 2
-EARLY = 2
+EARLY = 3
 HIDDEN = -1e30
 
 
@@ -127,17 +128,19 @@
             source.at[:, columns(h)], target.at[h], head_sem.at[number, h]
         )
 
-    def to_before(h):
+    def to_before(h, early=False):
         return [
             pltpu.make_async_remote_copy(
-                src_ref=source.at[h],
+                src_ref=origin.at[:, columns(h)] if early else source.at[h],
                 dst_ref=target.at[h],
                 send_sem=send_sem.at[number, h],
                 recv_sem=recv_sem.at[number, h],
                 device_id=before,
                 device_id_type=MESH,
             )
-            for number, (source, target) in enumerate(((q_own, q_next), (g_own, g_next)))
+            for number, (origin, source, target) in enumerate(
+                ((q_hbm, q_own, q_next), (g_hbm, g_own, g_next))
+            )
         ]
 
     def to_after(h):
@@ -153,14 +156,14 @@
     def keys_to_after(h):
         return [
             pltpu.make_async_remote_copy(
-                src_ref=source.at[h],
+                src_ref=source.at[:, columns(h)],
                 dst_ref=target.at[h],
                 send_sem=keys_send_sem.at[number, h],
                 recv_sem=keys_recv_sem.at[number, h],
                 device_id=after,
                 device_id_type=MESH,
             )
-            for number, (source, target) in enumerate(((k_own, k_before), (v_own, v_before)))
+            for number, (source, target) in enumerate(((k_hbm, k_before), (v_hbm, v_before)))
         ]
 
     def grads_to_before(h):
@@ -255,26 +258,9 @@
     greet(detours, relay_of_here)
     greet((core == 1) & has_after, relay_of_after)
 
-    for h in range(TURNED, TURNED + EARLY):
-        head_load(h, 0).start()
-        head_load(h, 1).start()
-    for h in range(TURNED):
-        head_load(h, 2).start()
-        head_load(h, 3).start()
     for copy in whole_loads:
         copy.start()
 
-    def start_loads(h, carry):
-        for number in range(4):
-            first = ((h < TURNED) | (h >= TURNED + EARLY)) if number < 2 else (h >= TURNED)
-
-            @pl.when(first)
-            def _():
-                head_load(h, number).start()
-
-        return carry
-
-    lax.fori_loop(0, heads, start_loads, 0)
     pl.semaphore_wait(
         barrier,
         has_before.astype(jnp.int32)
@@ -299,25 +285,27 @@
         h = TURNED + item
         return jnp.where(h < leaves - detoured, h, h + detoured)
 
-    def admit(h):
+    def admit(h, early=False):
         @pl.when(has_before)
         def _():
-            for copy in to_before(h):
+            for copy in to_before(h, early):
                 copy.start()
 
     for h in range(TURNED, TURNED + EARLY):
-        head_load(h, 0).wait()
-        head_load(h, 1).wait()
-        admit(h)
-    for h in range(TURNED):
-        head_load(h, 2).wait()
-        head_load(h, 3).wait()
-
-        @pl.when(has_after)
-        def _():
+        admit(h, True)
+
+    @pl.when(has_after)
+    def _():
+        for h in range(TURNED):
             for copy in keys_to_after(h):
                 copy.start()
 
+    def start_loads(h, carry):
+        for number in range(4):
+            head_load(h, number).start()
+        return carry
+
+    lax.fori_loop(0, heads, start_loads, 0)
 
     for copy in whole_loads:
         copy.wait()
@@ -351,11 +339,7 @@
 
     def settle(h, carry):
         for number in range(4):
-            waits = ((h < TURNED) | (h >= TURNED + EARLY)) if number < 2 else (h >= TURNED)
-
-            @pl.when(waits)
-            def _():
-                head_load(h, number).wait()
+            head_load(h, number).wait()
 
         return carry
 
@@ -474,23 +458,26 @@
         total = (dq_own[h] + dq_got[h].astype(jnp.float32)) * scale
         dq_out[:, columns(h)] = total.T.astype(jnp.bfloat16)
 
+    def leave(number):
+        if number == 0:
+            pl.semaphore_wait(ready_sem, 1)
+        for copy in to_relay(leaves - detoured + number):
+            copy.start()
+
+    @pl.when(detours & (z > 0))
+    def _():
+        for number in range(PLAIN):
+            leave(number)
+
     def lead(h, carry):
         local(h)
         return carry
 
     lax.fori_loop(0, TURNED + LEAD, lead, 0)
 
-    @pl.when(detours)
-    def _():
-        pl.semaphore_wait(ready_sem, 1)
-
-        def leave(h, carry):
-            for copy in to_relay(h):
-                copy.start()
-            return carry
-
-        lax.fori_loop(leaves - detoured, leaves, leave, 0)
-
+    @pl.when(detours & (z == 0))
+    def _():
+        leave(0)
 
     @pl.when(has_after)
     def _():
@@ -537,10 +524,16 @@
             for copy in grads_to_before(item + AHEAD - direct):
                 copy.start()
 
+        for number in range(1, WRAPPED):
+
+            @pl.when(detours & (z == 0) & (item == PACE * number - 1))
+            def _():
+                leave(number)
+
         for slot in range(WRAPPED + PLAIN):
             wanted, copies = forwards(slot)
 
-            @pl.when(wanted & (h == TURNED + FIRST + (slot + PLAIN) % (WRAPPED + PLAIN)))
+            @pl.when(wanted & (item == FORWARDED[slot]))
             def _():
                 for copy in arrived(slot):
                     copy.wait_recv()
@@ -584,8 +577,6 @@
 
     lax.fori_loop(TURNED, heads - LEAD, both, 0)
     lax.fori_loop(heads - LEAD, heads, shared_only, 0)
-    lax.fori_loop(heads - LAG, heads, lambda h, c: (finish(h), c)[1], 0)
-    lax.fori_loop(0, TURNED, lambda h, c: (finish_turned(h), c)[1], 0)
 
     def drain(h, carry):
         @pl.when(has_after & (h >= TURNED))
@@ -595,11 +586,6 @@
         @pl.when(has_after & (h < TURNED))
         def _():
             for copy in keys_to_after(h):
-                copy.wait_send()
-
-        @pl.when(has_before & (h < TURNED))
-        def _():
-            for copy in grads_to_before(h):
                 copy.wait_send()
 
         return carry
@@ -626,6 +612,26 @@
     @pl.when(has_before)
     def _():
         stats_copy.wait_send()
+
+    def finish_all_turned():
+        lax.fori_loop(0, TURNED, lambda h, c: (finish_turned(h), c)[1], 0)
+
+    @pl.when(core == 0)
+    def _():
+        finish_all_turned()
+
+    lax.fori_loop(heads - LAG, heads, lambda h, c: (finish(h), c)[1], 0)
+
+    @pl.when(core == 1)
+    def _():
+        finish_all_turned()
+
+
+    @pl.when(has_before)
+    def _():
+        for h in range(TURNED):
+            for copy in grads_to_before(h):
+                copy.wait_send()
 
 
 def write_out(*refs):

time: 54.2 us -> 53.8 us (level)
  Pallas kernels: 53.5 us -> 52.9 us
    pallas_call x1, Pallas kernels: 50.7 us -> 50.2 us  [local(): pl.pallas_call(functools.partial(kernel, groups, group_size, heads), out_...]
where the time goes in v5:
time: 53.8 us; the launch traced here: 53.6 us
  Pallas kernels  52.9 us (98%)
  between operations  0.64 us (1%)
    pallas_call x1, Pallas kernels, local(): pl.pallas_call(functools.partial(kernel, groups, group_size, heads), out_...  50.2 us
    pallas_call x1, Pallas kernels, local(): pl.pallas_call(write_out, out_shape=(jax.ShapeDtypeStruct((rows, model),...  2.73 us

profile of v5, /device:TPU:6, one launch (start us, length us, event | category | flops | bytes accessed | tf_op | source)
XLA Modules:
  0.0 53.6 jit_solution(15230537322793320887)
XLA Ops:
  0.6 50.2 %shard_map.103 = (bf16[512,2048]{1,0:T(8,128)(2,1)S(1)}, bf16[512,2048]{1,0:T(8,128)(2,1)S(1)}, bf16[512,2048]{1,0:T(8,128)(2,1)S(1)}) custom-call(bf16[512,2048]{1,0:T(8,128)(2,1)} %q_hbm.1, bf16[512,2048]{1,0:T(8,128)(2,1)} %k_hbm.1, bf16[512,2048]{1,0:T(8,128)(2,1)} %v_hbm.1, bf16[512,2048]{1,0:T(8,128)(2,1)} %o_hbm.1, bf16[512,2048]{1,0:T(8,128)(2,1)} %g_hbm.1, ...), custom_call_target="tpu_custom_call" | custom-call | tf_op jit(solution)/shard_map/pallas_call | solution.py:662
  50.8 2.7 %shard_map.104 = (bf16[512,2048]{1,0:T(8,128)(2,1)}, bf16[512,2048]{1,0:T(8,128)(2,1)}, bf16[512,2048]{1,0:T(8,128)(2,1)}) custom-call(bf16[512,2048]{1,0:T(8,128)(2,1)S(1)} %get-tuple-element.6.refs_0_, bf16[512,2048]{1,0:T(8,128)(2,1)S(1)} %get-tuple-element.7.refs_1_, bf16[512,2048]{1,0:T(8,128)(2,1)S(1)} %get-tuple-element.8.refs_2_), custom_call_target="tpu_custom_call" | custom-call | tf_op jit(solution)/shard_map/pallas_call | solution.py:715

commit v6 on v5

--- a/solution.py
+++ b/solution.py
@@ -226,8 +226,8 @@
         ]
 
     stats_copy = pltpu.make_async_remote_copy(
-        src_ref=stats_own,
-        dst_ref=stats_next,
+        src_ref=stats_own.at[8:],
+        dst_ref=stats_next.at[8:],
         send_sem=stats_sem.at[0],
         recv_sem=stats_sem.at[1],
         device_id=before,
@@ -314,7 +314,8 @@
         start_own[...].reshape(1, rows) - here * rows,
         positions - window_own[...].reshape(1, rows) + 1,
     )
-    stats_own[0:heads, :] = lse_own[...] * LOG2E
+    stats_own[0:TURNED, :] = lse_own[0:TURNED, :] * LOG2E
+    stats_own[8 : 5 + heads, :] = lse_own[TURNED:heads, :] * LOG2E
     model = heads * HEAD
     picks = (
         lax.broadcasted_iota(jnp.int32, (heads, model), 1) // HEAD
@@ -326,11 +327,11 @@
         )
         high = products.astype(jnp.bfloat16)
         low = (products - high.astype(jnp.float32)).astype(jnp.bfloat16)
-        stats_own[heads : 2 * heads, r : r + 128] = dot(picks, high, (1, 1)) + dot(
-            picks, low, (1, 1)
-        )
-    stats_own[2 * heads : 2 * heads + 8, :] = jnp.broadcast_to(
-        (lowest + rows).astype(jnp.float32), (8, rows)
+        sums = dot(picks, high, (1, 1)) + dot(picks, low, (1, 1))
+        stats_own[TURNED : 2 * TURNED, r : r + 128] = sums[0:TURNED]
+        stats_own[5 + heads : 2 + 2 * heads, r : r + 128] = sums[TURNED:heads]
+    stats_own[2 + 2 * heads : 8 + 2 * heads, :] = jnp.broadcast_to(
+        (lowest + rows).astype(jnp.float32), (6, rows)
     )
 
     @pl.when(has_before)
@@ -360,6 +361,12 @@
     bias[6] = hidden_where_not(key_at - half >= lowest[:, lo])
     bias[7] = hidden_where_not(key_at - rows >= lowest[:, lo])
     bias[8] = hidden_where_not(key_at - half >= lowest[:, hi])
+
+    def lse_row(h):
+        return jnp.where(h < TURNED, h, h + 5)
+
+    def delta_row(h):
+        return jnp.where(h < TURNED, h + TURNED, h + heads + 2)
 
     def pair_block(k, v, q, g, lse, delta, number):
         s = dot(k, q, (1, 1)) * (scale * LOG2E) + bias[number]
@@ -370,8 +377,8 @@
     def local(h):
         k, v, q, g = k_own[h], v_own[h], q_own[h], g_own[h]
         kt = k.T
-        lse = stats_own[pl.ds(h, 1), :]
-        delta = stats_own[pl.ds(heads + h, 1), :]
+        lse = stats_own[pl.ds(lse_row(h), 1), :]
+        delta = stats_own[pl.ds(delta_row(h), 1), :]
 
         def block(us, ts, number):
             return pair_block(k[us], v[us], q[ts], g[ts], lse[:, ts], delta[:, ts], number)
@@ -390,8 +397,8 @@
     def shared(h):
         k, v, q, g = k_own[h], v_own[h], q_next[h], g_next[h]
         kt = k.T
-        lse = stats_next[pl.ds(h, 1), :]
-        delta = stats_next[pl.ds(heads + h, 1), :]
+        lse = stats_next[pl.ds(lse_row(h), 1), :]
+        delta = stats_next[pl.ds(delta_row(h), 1), :]
 
         def block(us, ts, number):
             return pair_block(k[us], v[us], q[ts], g[ts], lse[:, ts], delta[:, ts], number)
@@ -419,8 +426,8 @@
             copy.wait_recv()
         k, v, q, g = k_before[h], v_before[h], q_own[h], g_own[h]
         kt = k.T
-        lse = stats_own[pl.ds(h, 1), :]
-        delta = stats_own[pl.ds(heads + h, 1), :]
+        lse = stats_own[pl.ds(lse_row(h), 1), :]
+        delta = stats_own[pl.ds(delta_row(h), 1), :]
 
         def block(us, ts, number):
             return pair_block(k[us], v[us], q[ts], g[ts], lse[:, ts], delta[:, ts], number)
@@ -502,7 +509,7 @@
 
         lax.fori_loop(0, heads, clear, 0)
 
-    bound = stats_next[2 * heads : 2 * heads + 1, :].astype(jnp.int32)
+    bound = stats_next[2 + 2 * heads : 3 + 2 * heads, :].astype(jnp.int32)
     bias[3] = hidden_where_not(key_at + half >= bound[:, lo])
     bias[4] = hidden_where_not(key_at >= bound[:, lo])
     bias[5] = hidden_where_not(key_at + half >= bound[:, hi])

time: 53.8 us -> 53.8 us (level)
  no operation moved by 1% of the time
where the time goes in v6:
time: 53.8 us; the launch traced here: 53.4 us
  Pallas kernels  52.8 us (98%)
  between operations  0.64 us (1%)
    pallas_call x1, Pallas kernels, local(): pl.pallas_call(functools.partial(kernel, groups, group_size, heads), out_...  50 us
    pallas_call x1, Pallas kernels, local(): pl.pallas_call(write_out, out_shape=(jax.ShapeDtypeStruct((rows, model),...  2.73 us

profile of v6, /device:TPU:6, one launch (start us, length us, event | category | flops | bytes accessed | tf_op | source)
XLA Modules:
  0.0 53.4 jit_solution(962716303312299976)
XLA Ops:
  0.6 50.0 %shard_map.103 = (bf16[512,2048]{1,0:T(8,128)(2,1)S(1)}, bf16[512,2048]{1,0:T(8,128)(2,1)S(1)}, bf16[512,2048]{1,0:T(8,128)(2,1)S(1)}) custom-call(bf16[512,2048]{1,0:T(8,128)(2,1)} %q_hbm.1, bf16[512,2048]{1,0:T(8,128)(2,1)} %k_hbm.1, bf16[512,2048]{1,0:T(8,128)(2,1)} %v_hbm.1, bf16[512,2048]{1,0:T(8,128)(2,1)} %o_hbm.1, bf16[512,2048]{1,0:T(8,128)(2,1)} %g_hbm.1, ...), custom_call_target="tpu_custom_call" | custom-call | tf_op jit(solution)/shard_map/pallas_call | solution.py:669
  50.7 2.7 %shard_map.104 = (bf16[512,2048]{1,0:T(8,128)(2,1)}, bf16[512,2048]{1,0:T(8,128)(2,1)}, bf16[512,2048]{1,0:T(8,128)(2,1)}) custom-call(bf16[512,2048]{1,0:T(8,128)(2,1)S(1)} %get-tuple-element.6.refs_0_, bf16[512,2048]{1,0:T(8,128)(2,1)S(1)} %get-tuple-element.7.refs_1_, bf16[512,2048]{1,0:T(8,128)(2,1)S(1)} %get-tuple-element.8.refs_2_), custom_call_target="tpu_custom_call" | custom-call | tf_op jit(solution)/shard_map/pallas_call | solution.py:722
